TPU v7x, 256 devices: a whole 4x4x8 slice. The times are simulated.
256 devices in a mesh: dp: 64 (over x_lo, z, y), tensor: 4 (over x_hi, core).
Axes of the slice: x: 4 (x_hi: 2, x_lo: 2; x = x_hi * 2 + x_lo), y: 4, z: 8, core: 2. Of those that a mesh axis runs over, the one named last changes fastest.
Arguments:
- queries: bfloat16 [64, 256, 4096], P('dp', None, 'tensor'), may hold values from -8 to 8
- keys: bfloat16 [64, 256, 512], P('dp', None, 'tensor'), may hold values from -8 to 8
- values: bfloat16 [64, 256, 512], P('dp', None, 'tensor'), may hold values from -6 to 6
- attn_out: bfloat16 [64, 256, 4096], P('dp', None, 'tensor'), may hold values from -6 to 6
- layer_in: bfloat16 [64, 256, 2560], P('dp', 'tensor'), may hold values from -16 to 16
- out_grad: bfloat16 [64, 256, 2560], P('dp', 'tensor'), may hold values from -16 to 16
- w_out: bfloat16 [4096, 2560], P('tensor', 'dp'), may hold values from -0.09375 to 0.09375
- w_value: bfloat16 [2560, 512], P('dp', 'tensor'), may hold values from -0.125 to 0.125
Outputs:
- query_grad: bfloat16 [64, 256, 4096], P('dp', None, 'tensor')
- key_grad: bfloat16 [64, 256, 512], P('dp', None, 'tensor')
- value_grad: bfloat16 [64, 256, 512], P('dp', None, 'tensor')
- input_grad: bfloat16 [64, 256, 2560], P('dp', 'tensor')
- out_weight_grad: float32 [4096, 2560], P('tensor', 'dp')
- value_weight_grad: float32 [2560, 512], P('dp', 'tensor')
All inputs are finite; a program needn't handle non-finite values.
Results may differ from a plain program's by a relative error of at most 0.015.
Values may be sent and summed in bfloat16 or wider, within the bound.
No kernel may reach another device: no remote copies, remote signals or barrier semaphores. Data moves between devices by JAX's collectives and lax.ppermute only.
A program may use at most 128 MiB of HBM per device.

v0:
```python
import functools

import jax
import jax.numpy as jnp
from jax import lax
from jax.experimental import pallas as pl
from jax.experimental.pallas import tpu as pltpu
from jax.sharding import Mesh
from jax.sharding import PartitionSpec as P

HEAD = 128
SIZES = {"xl": 2, "z": 8, "y": 4, "xh": 2, "c": 2}
DP = ("xl", "z", "y")
TENSOR = ("xh", "c")
F32 = jnp.float32
BF16 = jnp.bfloat16


def shift(array, axis, by):
    count = SIZES[axis]
    return lax.ppermute(array, axis, [(i, (i + by) % count) for i in range(count)])


LAST = (((1,), (1,)), ((), ()))
FIRST = (((0,), (0,)), ((), ()))


def after(array, *earlier):
    return lax.optimization_barrier((array,) + earlier)[0]


LIGHT = pl.CostEstimate(flops=1, bytes_accessed=1, transcendentals=0)
SHORT = pl.CostEstimate(flops=4 * 10**9, bytes_accessed=10**7, transcendentals=0)


def limits():
    return pltpu.CompilerParams(vmem_limit_bytes=16 * 1024 * 1024)


def whole(shape):
    return pl.BlockSpec(shape, lambda *_: (0,) * len(shape))


def probs_kernel(scale, heads, q_ref, k_ref, probs_ref):
    keys = k_ref[...]
    seq = keys.shape[0]
    rows = lax.broadcasted_iota(jnp.int32, (seq, seq), 0)
    cols = lax.broadcasted_iota(jnp.int32, (seq, seq), 1)
    for h in range(heads):
        q = q_ref[:, h * HEAD : (h + 1) * HEAD]
        scores = lax.dot_general(keys, q, LAST, preferred_element_type=F32) * scale
        scores = jnp.where(cols >= rows, scores, -jnp.inf)
        exponent = jnp.exp(scores - jnp.max(scores, axis=0, keepdims=True))
        probs_ref[h] = (exponent / jnp.sum(exponent, axis=0, keepdims=True)).astype(BF16)


def probabilities(q, k):
    seq, width = q.shape
    heads = 2
    count = width // HEAD
    return pl.pallas_call(
        functools.partial(probs_kernel, HEAD**-0.5, heads),
        grid=(count // heads,),
        in_specs=[pl.BlockSpec((seq, heads * HEAD), lambda i: (0, i)), whole((seq, HEAD))],
        out_specs=pl.BlockSpec((heads, seq, seq), lambda i: (i, 0, 0)),
        out_shape=jax.ShapeDtypeStruct((count, seq, seq), BF16),
        cost_estimate=LIGHT,
        compiler_params=limits(),
    )(q, k)


def gather_rows(position, c, near_ref, far_ref, rows_ref):
    count = near_ref.shape[0] // 2
    rows = near_ref.shape[1]
    for k in range(count):
        for xh in range(2):
            index = (position + count - k) % count * 2 + xh
            start = (k * 2 + xh) * 2 * rows
            rows_ref[pl.ds(pl.multiple_of(start + c * rows, rows), rows)] = near_ref[index]
            rows_ref[pl.ds(pl.multiple_of(start + (1 - c) * rows, rows), rows)] = far_ref[index]


def out_kernel(place, near_ref, far_ref, *refs):
    ao_refs, (part_ref, grads_ref) = refs[:-2], refs[-2:]
    step = pl.program_id(0)
    seq = ao_refs[0].shape[0]

    @pl.when(step == 0)
    def _():
        gather_rows(place[2], place[1], near_ref, far_ref, grads_ref)

    chunk = part_ref.shape[0]
    span = pl.ds(pl.multiple_of(step * chunk, chunk), chunk)
    total = jnp.zeros(part_ref.shape, F32)
    for k, ao_ref in enumerate(ao_refs):
        total += lax.dot_general(
            grads_ref[k * seq : (k + 1) * seq, span], ao_ref[...], FIRST, preferred_element_type=F32
        )
    part_ref[...] = total.astype(BF16)


def out_part(place, near, far, aos):
    seq, width = aos[0].shape
    feats = near.shape[2]
    chunk = feats // 5
    return pl.pallas_call(
        out_kernel,
        grid_spec=pltpu.PrefetchScalarGridSpec(
            num_scalar_prefetch=1,
            grid=(feats // chunk,),
            in_specs=[whole(near.shape), whole(far.shape)] + [whole(ao.shape) for ao in aos],
            out_specs=pl.BlockSpec((chunk, width), lambda i, place: (i, 0)),
            scratch_shapes=[pltpu.VMEM((len(aos) * seq, feats), BF16)],
        ),
        out_shape=jax.ShapeDtypeStruct((feats, width), BF16),
        cost_estimate=LIGHT,
        compiler_params=limits(),
    )(place, near, far, *aos)


def head_kernel(offsets, place, near_ref, far_ref, *refs):
    n_z = len(offsets)
    w_refs, wv_refs, refs = refs[:n_z], refs[n_z : 2 * n_z], refs[2 * n_z :]
    own_ref, send_refs, (wv_ref, grads_ref, w_all) = refs[0], refs[1:-3], refs[-3:]
    depth = w_refs[0].shape[0]

    def in_order(pieces, ref):
        for offset, piece in zip(offsets, pieces):
            start = (place[3] + offset + n_z) % n_z * depth
            ref[pl.ds(pl.multiple_of(start, depth), depth)] = piece[...]

    @pl.when(pl.program_id(0) == 0)
    def _():
        gather_rows(place[2], place[1], near_ref, far_ref, grads_ref)
        in_order(wv_refs, wv_ref)

    in_order(w_refs, w_all)
    seq = own_ref.shape[0]
    product = jnp.dot(grads_ref[...], w_all[...], preferred_element_type=F32)
    own_ref[...] = product[:seq]
    for k, ref in enumerate(send_refs):
        ref[...] = product[(k + 1) * seq : (k + 2) * seq].astype(BF16)


def head_parts(place, near, far, pieces, seq, width):
    feats = near.shape[2]
    count = near.shape[0] // 2
    block = 256
    depth = feats // len(pieces)
    wide = pl.BlockSpec((seq, block), lambda i, place: (0, i))
    return pl.pallas_call(
        functools.partial(head_kernel, tuple(pieces)),
        grid_spec=pltpu.PrefetchScalarGridSpec(
            num_scalar_prefetch=1,
            grid=(width // block,),
            in_specs=[whole(near.shape), whole(far.shape)]
            + [pl.BlockSpec((depth, block), lambda i, place: (0, i))] * len(pieces)
            + [pl.BlockSpec((depth, HEAD), lambda i, place: (0, width // HEAD))] * len(pieces),
            out_specs=[wide] * count + [whole((feats, HEAD))],
            scratch_shapes=[pltpu.VMEM((count * seq, feats), BF16), pltpu.VMEM((feats, block), BF16)],
        ),
        out_shape=[jax.ShapeDtypeStruct((seq, width), F32)]
        + [jax.ShapeDtypeStruct((seq, width), BF16)] * (count - 1)
        + [jax.ShapeDtypeStruct((feats, HEAD), BF16)],
        cost_estimate=LIGHT,
        compiler_params=limits(),
    )(place, near, far, *pieces.values(), *pieces.values())


def grad_kernel(heads, probs_ref, own_ref, *refs):
    recv_refs, (grad_ref, dv_ref) = refs[:-2], refs[-2:]
    total = jnp.zeros(dv_ref.shape, F32)
    for h in range(heads):
        span = slice(h * HEAD, (h + 1) * HEAD)
        grad = own_ref[:, span]
        for ref in recv_refs:
            grad += ref[:, span].astype(F32)
        grad = grad.astype(BF16)
        grad_ref[:, span] = grad
        total += jnp.dot(probs_ref[h], grad, preferred_element_type=F32)
    dv_ref[...] = total.astype(BF16)


def head_gradient(probs, own, recv):
    seq, width = own.shape
    return pl.pallas_call(
        functools.partial(grad_kernel, width // HEAD),
        out_shape=[jax.ShapeDtypeStruct((seq, width), BF16), jax.ShapeDtypeStruct((seq, HEAD), BF16)],
        cost_estimate=SHORT,
        compiler_params=limits(),
    )(probs, own, *recv)


def score_kernel(scale, heads, q_ref, k_ref, v_ref, ao_ref, grad_ref, dq_ref, dk_ref, dk_sum):
    step = pl.program_id(0)

    @pl.when(step == 0)
    def _():
        dk_sum[...] = jnp.zeros_like(dk_sum)

    keys = k_ref[...]
    vals = v_ref[...]
    seq = keys.shape[0]
    rows = lax.broadcasted_iota(jnp.int32, (seq, seq), 0)
    cols = lax.broadcasted_iota(jnp.int32, (seq, seq), 1)
    dk_here = jnp.zeros(dk_sum.shape, F32)
    for h in range(heads):
        span = slice(h * HEAD, (h + 1) * HEAD)
        q = q_ref[:, span]
        grad = grad_ref[:, span]
        scores = lax.dot_general(q, keys, LAST, preferred_element_type=F32) * scale
        scores = jnp.where(rows >= cols, scores, -jnp.inf)
        exponent = jnp.exp(scores - jnp.max(scores, axis=1, keepdims=True))
        probs = exponent / jnp.sum(exponent, axis=1, keepdims=True)
        prob_grad = lax.dot_general(grad, vals, LAST, preferred_element_type=F32)
        row_dot = jnp.sum(grad.astype(F32) * ao_ref[:, span].astype(F32), axis=1, keepdims=True)
        score_grad = (probs * (prob_grad - row_dot)).astype(BF16)
        dq_ref[:, span] = (jnp.dot(score_grad, keys, preferred_element_type=F32) * scale).astype(BF16)
        dk_here += lax.dot_general(score_grad, q, FIRST, preferred_element_type=F32)
    dk_sum[...] += dk_here

    @pl.when(step == pl.num_programs(0) - 1)
    def _():
        dk_ref[...] = (dk_sum[...] * scale).astype(BF16)


def score_gradients(q, k, v, ao, grad):
    seq, width = q.shape
    heads = 2
    count = width // HEAD
    wide = pl.BlockSpec((seq, heads * HEAD), lambda i: (0, i))
    narrow = whole((seq, HEAD))
    return pl.pallas_call(
        functools.partial(score_kernel, HEAD**-0.5, heads),
        grid=(count // heads,),
        in_specs=[wide, narrow, narrow, wide, wide],
        out_specs=[wide, narrow],
        out_shape=[jax.ShapeDtypeStruct((seq, width), BF16), jax.ShapeDtypeStruct((seq, HEAD), BF16)],
        scratch_shapes=[pltpu.VMEM((seq, HEAD), F32)],
        cost_estimate=LIGHT,
        compiler_params=limits(),
    )(q, k, v, ao, grad)


def input_kernel(n_xl, n_z, cols, place, dv_ref, *refs):
    wv_refs, (keep_ref, give_ref, wv_all) = refs[:-3], refs[-3:]
    c, y, n_y = place[1], place[2], len(wv_refs)
    for k, ref in enumerate(wv_refs):
        from_y = (y + n_y - k) % n_y
        for z in range(n_z):
            for xl in range(n_xl):
                start = (xl * n_z + z) * n_y + from_y
                block = ref[(z * n_xl + xl) * cols : (z * n_xl + xl + 1) * cols].astype(F32)
                wv_all[pl.ds(pl.multiple_of(start * cols, 8), cols)] = block
    wv = wv_all[...].astype(BF16)
    for xh in range(2):
        keep_ref[xh] = lax.dot_general(dv_ref[xh, c], wv, LAST, preferred_element_type=F32)
        give = lax.dot_general(dv_ref[xh, 1 - c], wv, LAST, preferred_element_type=F32)
        give_ref[xh] = give.astype(BF16)


def input_parts(place, dv, wvs, n_xl, n_z, cols):
    rows = dv.shape[2]
    feats = len(wvs) * wvs[0].shape[0]
    shape = (2, rows, feats)
    return pl.pallas_call(
        functools.partial(input_kernel, n_xl, n_z, cols),
        grid_spec=pltpu.PrefetchScalarGridSpec(
            num_scalar_prefetch=1,
            grid=(1,),
            in_specs=[whole(dv.shape)] + [whole(wv.shape) for wv in wvs],
            out_specs=[whole(shape), whole(shape)],
            scratch_shapes=[pltpu.VMEM((feats, HEAD), F32)],
        ),
        out_shape=[jax.ShapeDtypeStruct(shape, F32), jax.ShapeDtypeStruct(shape, BF16)],
        cost_estimate=SHORT,
        compiler_params=limits(),
    )(place, dv, *wvs)


def value_kernel(cols, scale, place, near_ref, far_ref, *refs):
    dv_refs, part_refs, rows_ref = refs[:2], refs[2:-1], refs[-1]
    y = place[2]
    gather_rows(place[0], place[1], near_ref, far_ref, rows_ref)
    seq = dv_refs[0].shape[0]
    total = jnp.zeros((rows_ref.shape[1], HEAD), F32)
    for k, ref in enumerate(dv_refs):
        total += lax.dot_general(rows_ref[k * seq : (k + 1) * seq], ref[...], FIRST, preferred_element_type=F32)
    n_y = len(part_refs)
    for to_y in range(n_y):
        for k, ref in enumerate(part_refs):

            @pl.when((y + k) % n_y == to_y)
            def _():
                for z in range(ref.shape[0]):
                    start = (z * n_y + to_y) * cols
                    ref[z] = (total[start : start + cols] * scale).astype(BF16)


def value_parts(place, near, far, dvs, n_y, cols, scale):
    half = near.shape[2]
    shape = (half // cols // n_y, cols, HEAD)
    return pl.pallas_call(
        functools.partial(value_kernel, cols, scale),
        grid_spec=pltpu.PrefetchScalarGridSpec(
            num_scalar_prefetch=1,
            grid=(1,),
            in_specs=[whole(array.shape) for array in [near, far] + dvs],
            out_specs=[whole(shape)] * n_y,
            scratch_shapes=[pltpu.VMEM((len(dvs) * dvs[0].shape[0], half), BF16)],
        ),
        out_shape=[jax.ShapeDtypeStruct(shape, BF16)] * n_y,
        cost_estimate=SHORT,
        compiler_params=limits(),
    )(place, near, far, *dvs)


def split_kernel(rows_ref, halves_ref):
    half = halves_ref.shape[2]
    for i in range(halves_ref.shape[0]):
        halves_ref[i] = rows_ref[:, i // 2 * half : (i // 2 + 1) * half]


def split(array, count):
    rows, feats = array.shape
    shape = (2 * count, rows, feats // count)
    return pl.pallas_call(
        split_kernel,
        in_specs=[whole(array.shape)],
        out_specs=whole(shape),
        out_shape=jax.ShapeDtypeStruct(shape, BF16),
        cost_estimate=LIGHT,
        compiler_params=limits(),
    )(array)


def for_each(parts):
    both = jnp.broadcast_to(parts[:, None], (parts.shape[0], 2) + parts.shape[1:])
    return both.reshape((parts.shape[0] * 2,) + parts.shape[1:])


def on_device(queries, keys, values, attn_out, layer_in, out_grad, w_out, w_value):
    xl, z, y, xh, c = (lax.axis_index(a) for a in ("xl", "z", "y", "xh", "c"))
    place = jnp.stack([xl, c, y, z]).astype(jnp.int32)
    n_xl, n_z, n_y = SIZES["xl"], SIZES["z"], SIZES["y"]
    n_dp = n_xl * n_z * n_y
    q, k, v, ao, li, og = (a[0] for a in (queries, keys, values, attn_out, layer_in, out_grad))
    seq, width = q.shape
    rows, feats = og.shape
    quarter = feats // n_y
    cols = feats // n_dp

    shard = jnp.concatenate([w_out.T, w_value], axis=1)
    other = shift(shard, "xl", 1)
    plane = jnp.where(xl == 0, jnp.concatenate([shard, other]), jnp.concatenate([other, shard]))
    aos = [ao] + [shift(ao, "y", step) for step in range(1, n_y)]
    pieces = {0: plane}
    for step in range(1, n_z // 2):
        if step == 3:
            pieces[-2], pieces[2], _, _ = lax.optimization_barrier((pieces[-2], pieces[2], aos[1], aos[3]))
        pieces[-step] = shift(pieces[1 - step], "z", 1)
        pieces[step] = shift(pieces[step - 1], "z", -1)
    pieces[-n_z // 2] = shift(after(pieces[1 - n_z // 2], aos[2]), "z", 1)

    by_y = og.reshape(rows, n_xl, n_z, n_y, cols).transpose(3, 0, 2, 1, 4).reshape(n_y, rows, quarter)
    near = lax.all_to_all(after(for_each(by_y), plane), ("y", "xh"), 0, 0, tiled=True)
    near = after(near, pieces[-1], pieces[1])
    far = shift(near, "c", 1)

    li_near = lax.all_to_all(after(split(li, n_xl), near), ("xl", "xh"), 0, 0, tiled=True)
    li_near = after(li_near, pieces[-3], pieces[3])
    li_far = shift(li_near, "c", 1)

    own, *sends, wv = head_parts(place, after(near, li_far), far, pieces, seq, width)
    recv = [shift(send, "y", -step - 1) for step, send in enumerate(sends)]
    probs = probabilities(after(q, sends[0]), k)

    part = out_part(place, after(near, sends[0]), far, aos)
    parts = lax.all_to_all(part.reshape(n_z, n_xl * cols, width), "z", 0, 0, tiled=True)
    part = jnp.sum(parts.astype(F32), axis=0).astype(BF16)
    wv, probs, *recv = lax.optimization_barrier((wv, probs, *recv))
    wvs = [wv] + [shift(wv, "y", step) for step in range(1, n_y)]
    head_grad, value_grad = head_gradient(probs, own, recv)
    dvs = [value_grad, shift(value_grad, "xl", 1)]

    value_part = value_parts(place, li_near, li_far, dvs, n_y, cols, 1 / n_dp)
    first_part = value_part[0]
    value_part = [value_part[0]] + [shift(value_part[step], "y", step) for step in range(1, n_y)]
    value_part = sum(piece.astype(F32) for piece in value_part).astype(BF16)

    keep, give = input_parts(place, value_grad.reshape(2, 2, rows, HEAD), wvs, n_xl, n_z, cols)
    give = shift(after(give, first_part), "c", 1)

    def sum_of(i):
        return lax.dynamic_index_in_dim(keep, i, 0, False) + lax.dynamic_index_in_dim(give, i, 0, False).astype(F32)

    last = shift(sum_of(1 - xh).astype(BF16), "xh", 1)
    value_part = lax.all_to_all(after(value_part, parts), "z", 0, 0, tiled=True)

    part = part.reshape(n_xl, cols, width)
    mine = lax.dynamic_index_in_dim(part, xl, 0, False).astype(F32)
    other = shift(lax.dynamic_index_in_dim(part, 1 - xl, 0, False), "xl", 1)

    query_grad, key_grad = score_gradients(q, k, v, ao, after(head_grad, other))
    input_grad = (sum_of(xh) + after(last, key_grad).astype(F32)).astype(BF16)
    out_weight_grad = ((mine + other.astype(F32)) / n_dp).T
    value_weight_grad = jnp.sum(value_part.astype(F32), axis=0)

    return (
        query_grad[None],
        key_grad[None],
        value_grad[None],
        input_grad[None],
        out_weight_grad,
        value_weight_grad,
    )


def solution(mesh):
    fine = Mesh(mesh.devices.reshape(tuple(SIZES.values())), tuple(SIZES))
    heads = P(DP, None, TENSOR)
    tokens = P(DP, TENSOR, None)
    return jax.shard_map(
        on_device,
        mesh=fine,
        in_specs=(heads, heads, heads, heads, tokens, tokens, P(TENSOR, DP), P(DP, TENSOR)),
        out_specs=(heads, heads, heads, tokens, P(TENSOR, DP), P(DP, TENSOR)),
        check_vma=False,
    )
```

profile of v0, /device:TPU:2, one launch (start us, length us, event | category | flops | bytes accessed | tf_op | source)
XLA Modules:
  0.0 133.4 jit_solution(2136694759186261811)
XLA Ops:
  1.5 2.3 %collective-permute-start = (bf16[40,1152]{1,0:T(8,128)(2,1)S(1)}, bf16[40,1152]{1,0:T(8,128)(2,1)S(1)}, u32[]{:S(2)}, u32[]{:S(2)}) collective-permute-start(bf16[40,1152]{1,0:T(8,128)(2,1)S(1)} %pad_maximum_fusion), channel_id=1, source_target_pairs={{0,128},{128,0},{1,129},{129,1},{2,130},{130,2},{3,131},{131,3},{4... | collective-permute-start | bytes 276488 | tf_op jit(solution)/shard_map/ppermute | solution.py:21
  7.4 5.8 %all-to-all-start = ((bf16[8,64,640]{2,1,0:T(8,128)(2,1)}), bf16[8,64,640]{2,1,0:T(8,128)(2,1)S(1)}, u32[]{:S(2)}, u32[]{:S(2)}) async-start(bf16[8,64,640]{2,1,0:T(8,128)(2,1)} %bitcast.11), calls=%async_computation | async-start | bytes 1310720 | tf_op jit(solution)/shard_map/all_to_all | solution.py:366
  13.1 3.2 %collective-permute-start.6 = (bf16[256,1024]{1,0:T(8,128)(2,1)S(1)}, bf16[256,1024]{1,0:T(8,128)(2,1)S(1)}, u32[]{:S(2)}, u32[]{:S(2)}) collective-permute-start(bf16[256,1024]{1,0:T(8,128)(2,1)S(1)} %bitcast.40), channel_id=1, source_target_pairs={{0,12},{4,0},{8,4},{12,8},{1,13},{5,1},{9,5},{13,9},{2,14},{6,2},{... | collective-permute-start | bytes 1572872 | tf_op jit(solution)/shard_map/ppermute | solution.py:21
  16.4 5.9 %collective-permute-start.2 = (bf16[80,1152]{1,0:T(8,128)(2,1)S(1)}, bf16[80,1152]{1,0:T(8,128)(2,1)S(1)}, u32[]{:S(2)}, u32[]{:S(2)}) collective-permute-start(bf16[80,1152]{1,0:T(8,128)(2,1)S(1)} %maximum_select_fusion.refs_0_.refs_8_), channel_id=1, source_target_pairs={{0,112},{16,0},{32,16},{48,32},{64,48},{80,64},{96,80},{112,96},{1... | collective-permute-start | bytes 552968 | tf_op jit(solution)/shard_map/ppermute | solution.py:21
  23.1 2.2 %collective-permute-done.2.refs_2_.refs_10_ = bf16[80,1152]{1,0:T(8,128)(2,1)S(1)} collective-permute-done((bf16[80,1152]{1,0:T(8,128)(2,1)S(1)}, bf16[80,1152]{1,0:T(8,128)(2,1)S(1)}, u32[]{:S(2)}, u32[]{:S(2)}) %collective-permute-start.2) | collective-permute-done | bytes 184352 | tf_op jit(solution)/shard_map/ppermute | solution.py:21
  25.3 3.7 %collective-permute-done.1.refs_1_.refs_9_ = bf16[80,1152]{1,0:T(8,128)(2,1)S(1)} collective-permute-done((bf16[80,1152]{1,0:T(8,128)(2,1)S(1)}, bf16[80,1152]{1,0:T(8,128)(2,1)S(1)}, u32[]{:S(2)}, u32[]{:S(2)}) %collective-permute-start.1) | collective-permute-done | bytes 184352 | tf_op jit(solution)/shard_map/ppermute | solution.py:21
  29.0 5.7 %all-to-all-start.1 = ((bf16[4,64,1280]{2,1,0:T(8,128)(2,1)}), bf16[4,64,1280]{2,1,0:T(8,128)(2,1)}, u32[]{:S(2)}, u32[]{:S(2)}) async-start(bf16[4,64,1280]{2,1,0:T(8,128)(2,1)} %shard_map.127), calls=%async_computation.1 | async-start | bytes 1310720 | tf_op jit(solution)/shard_map/all_to_all | solution.py:370
  34.7 2.2 %collective-permute-start.4 = (bf16[80,1152]{1,0:T(8,128)(2,1)S(1)}, bf16[80,1152]{1,0:T(8,128)(2,1)S(1)}, u32[]{:S(2)}, u32[]{:S(2)}) collective-permute-start(bf16[80,1152]{1,0:T(8,128)(2,1)S(1)} %collective-permute-done.2.refs_2_.refs_10_), channel_id=1, source_target_pairs={{0,112},{16,0},{32,16},{48,32},{64,48},{80,64},{96,80},{112,96},{1... | collective-permute-start | bytes 552968 | tf_op jit(solution)/shard_map/ppermute | solution.py:21
  36.9 3.3 %collective-permute-done.4.refs_4_.refs_12_ = bf16[80,1152]{1,0:T(8,128)(2,1)S(1)} collective-permute-done((bf16[80,1152]{1,0:T(8,128)(2,1)S(1)}, bf16[80,1152]{1,0:T(8,128)(2,1)S(1)}, u32[]{:S(2)}, u32[]{:S(2)}) %collective-permute-start.4) | collective-permute-done | bytes 184352 | tf_op jit(solution)/shard_map/ppermute | solution.py:21
  40.2 3.5 %collective-permute-done.3.refs_3_.refs_11_ = bf16[80,1152]{1,0:T(8,128)(2,1)S(1)} collective-permute-done((bf16[80,1152]{1,0:T(8,128)(2,1)S(1)}, bf16[80,1152]{1,0:T(8,128)(2,1)S(1)}, u32[]{:S(2)}, u32[]{:S(2)}) %collective-permute-start.3) | collective-permute-done | bytes 184352 | tf_op jit(solution)/shard_map/ppermute | solution.py:21
  45.3 3.2 %collective-permute-start.8 = (bf16[80,1152]{1,0:T(8,128)(2,1)S(1)}, bf16[80,1152]{1,0:T(8,128)(2,1)S(1)}, u32[]{:S(2)}, u32[]{:S(2)}) collective-permute-start(bf16[80,1152]{1,0:T(8,128)(2,1)S(1)} %collective-permute-done.4.refs_4_.refs_12_), channel_id=1, source_target_pairs={{0,112},{16,0},{32,16},{48,32},{64,48},{80,64},{96,80},{112,96},{1... | collective-permute-start | bytes 552968 | tf_op jit(solution)/shard_map/ppermute | solution.py:21
  49.0 3.1 %collective-permute-done.7.refs_5_.refs_13_ = bf16[80,1152]{1,0:T(8,128)(2,1)S(1)} collective-permute-done((bf16[80,1152]{1,0:T(8,128)(2,1)S(1)}, bf16[80,1152]{1,0:T(8,128)(2,1)S(1)}, u32[]{:S(2)}, u32[]{:S(2)}) %collective-permute-start.7) | collective-permute-done | bytes 184352 | tf_op jit(solution)/shard_map/ppermute | solution.py:21
  52.5 6.8 %collective-permute-done.11.refs_2_ = bf16[256,1024]{1,0:T(8,128)(2,1)} collective-permute-done((bf16[256,1024]{1,0:T(8,128)(2,1)S(1)}, bf16[256,1024]{1,0:T(8,128)(2,1)}, u32[]{:S(2)}, u32[]{:S(2)}) %collective-permute-start.11) | collective-permute-done | bytes 524320 | tf_op jit(solution)/shard_map/ppermute | solution.py:21
  59.4 6.7 %collective-permute-done.12.refs_7_.refs_15_ = bf16[80,1152]{1,0:T(8,128)(2,1)S(1)} collective-permute-done((bf16[80,1152]{1,0:T(8,128)(2,1)S(1)}, bf16[80,1152]{1,0:T(8,128)(2,1)S(1)}, u32[]{:S(2)}, u32[]{:S(2)}) %collective-permute-start.12) | collective-permute-done | bytes 184352 | tf_op jit(solution)/shard_map/ppermute | solution.py:21
  66.1 5.3 %shard_map.128 = (f32[256,1024]{1,0:T(8,128)S(1)}, bf16[256,1024]{1,0:T(8,128)(2,1)}, bf16[256,1024]{1,0:T(8,128)(2,1)}, bf16[256,1024]{1,0:T(8,128)(2,1)}, bf16[640,128]{1,0:T(8,128)(2,1)S(1)}) custom-call(s32[4]{0:T(128)S(1)} %pad_add_fusion.place, bf16[8,64,640]{2,1,0:T(8,128)(2,1)S(1)} %all-to-all-done.near_ref, ...), custom_call_target="tpu_custom_call" | custom-call | flops 1 | bytes 1 | tf_op jit(solution)/shard_map/pallas_call | solution.py:151
  73.3 2.0 %collective-permute-start.13 = (bf16[256,1024]{1,0:T(8,128)(2,1)}, bf16[256,1024]{1,0:T(8,128)(2,1)}, u32[]{:S(2)}, u32[]{:S(2)}) collective-permute-start(bf16[256,1024]{1,0:T(8,128)(2,1)} %get-tuple-element.49), channel_id=1, source_target_pairs={{0,12},{4,0},{8,4},{12,8},{1,13},{5,1},{9,5},{13,9},{2,14},{6,2},{... | collective-permute-start | bytes 1572872 | tf_op jit(solution)/shard_map/ppermute | solution.py:21
  75.4 5.3 %shard_map.131 = bf16[640,1024]{1,0:T(8,128)(2,1)} custom-call(s32[4]{0:T(128)S(1)} %pad_add_fusion.place, bf16[8,64,640]{2,1,0:T(8,128)(2,1)S(1)} %all-to-all-done.near_ref, bf16[8,64,640]{2,1,0:T(8,128)(2,1)S(1)} %collective-permute-done.10.far_ref, bf16[256,1024]{1,0:T(8,128)(2,1)S(1)} %bitcast.43, bf16[256,1024]{1,0:T(8,128)(2,1)S(1)} %copy-done.5, ...), custom_call_target="tpu_custom_call" | custom-call | flops 1 | bytes 1 | tf_op jit(solution)/shard_map/pallas_call | solution.py:106
  80.7 4.4 %all-to-all-start.2 = ((bf16[8,80,1024]{2,1,0:T(8,128)(2,1)}), bf16[8,80,1024]{2,1,0:T(8,128)(2,1)}, u32[]{:S(2)}, u32[]{:S(2)}) async-start(bf16[8,80,1024]{2,1,0:T(8,128)(2,1)} %bitcast.14), calls=%async_computation.2 | async-start | bytes 2621440 | tf_op jit(solution)/shard_map/all_to_all | solution.py:379
  86.7 4.3 %collective-permute-done.15.refs_2_ = bf16[256,1024]{1,0:T(8,128)(2,1)} collective-permute-done((bf16[256,1024]{1,0:T(8,128)(2,1)}, bf16[256,1024]{1,0:T(8,128)(2,1)}, u32[]{:S(2)}, u32[]{:S(2)}) %collective-permute-start.15) | collective-permute-done | bytes 524320 | tf_op jit(solution)/shard_map/ppermute | solution.py:21
  91.0 2.5 %shard_map.130 = (bf16[256,1024]{1,0:T(8,128)(2,1)S(1)}, bf16[256,128]{1,0:T(8,128)(2,1)}) custom-call(bf16[8,256,256]{2,1,0:T(8,128)(2,1)S(1)} %shard_map.129.probs_ref, f32[256,1024]{1,0:T(8,128)S(1)} %copy-done.10, bf16[256,1024]{1,0:T(8,128)(2,1)} %collective-permute-done.13.refs_0_, bf16[256,1024]{1,0:T(8,128)(2,1)} %collective-permute-done.14.refs_1_, ...), custom_call_target="tpu_custom_call" | custom-call | flops 4000000000 | bytes 10000000 | tf_op jit(solution)/shard_map/pallas_call | solution.py:186
  94.8 2.0 %collective-permute-start.18 = (bf16[640,128]{1,0:T(8,128)(2,1)S(1)}, bf16[640,128]{1,0:T(8,128)(2,1)S(1)}, u32[]{:S(2)}, u32[]{:S(2)}) collective-permute-start(bf16[640,128]{1,0:T(8,128)(2,1)S(1)} %get-tuple-element.64.refs_0_), channel_id=1, source_target_pairs={{0,8},{4,12},{8,0},{12,4},{1,9},{5,13},{9,1},{13,5},{2,10},{6,14},... | collective-permute-start | bytes 491528 | tf_op jit(solution)/shard_map/ppermute | solution.py:21
  98.8 3.3 %shard_map.134 = (bf16[8,40,128]{2,1,0:T(8,128)(2,1)S(1)}, bf16[8,40,128]{2,1,0:T(8,128)(2,1)}, bf16[8,40,128]{2,1,0:T(8,128)(2,1)}, bf16[8,40,128]{2,1,0:T(8,128)(2,1)}) custom-call(s32[4]{0:T(128)S(1)} %pad_add_fusion.place, bf16[4,64,1280]{2,1,0:T(8,128)(2,1)} %all-to-all-done.1.near_ref, bf16[4,64,1280]{2,1,0:T(8,128)(2,1)} %collective-permute-done.9.far_ref, ...), custom_call_target="tpu_custom_call" | custom-call | flops 4000000000 | bytes 10000000 | tf_op jit(solution)/shard_map/pallas_call | solution.py:303
  103.3 2.5 %shard_map.133 = (f32[2,64,2560]{2,1,0:T(8,128)S(1)}, bf16[2,64,2560]{2,1,0:T(8,128)(2,1)}) custom-call(s32[4]{0:T(128)S(1)} %pad_add_fusion.place, bf16[2,2,64,128]{3,2,1,0:T(8,128)(2,1)S(1)} %bitcast.50, bf16[640,128]{1,0:T(8,128)(2,1)S(1)} %get-tuple-element.64.refs_0_, bf16[640,128]{1,0:T(8,128)(2,1)S(1)} %collective-permute-done.17.refs_1_, ...), custom_call_target="tpu_custom_call" | custom-call | flops 4000000000 | bytes 10000000 | tf_op jit(solution)/shard_map/pallas_call | solution.py:266
  106.4 1.7 %collective-permute-start.24 = (bf16[8,40,128]{2,1,0:T(8,128)(2,1)}, bf16[8,40,128]{2,1,0:T(8,128)(2,1)}, u32[]{:S(2)}, u32[]{:S(2)}) collective-permute-start(bf16[8,40,128]{2,1,0:T(8,128)(2,1)} %get-tuple-element.71), channel_id=1, source_target_pairs={{0,8},{4,12},{8,0},{12,4},{1,9},{5,13},{9,1},{13,5},{2,10},{6,14},... | collective-permute-start | bytes 245768 | tf_op jit(solution)/shard_map/ppermute | solution.py:21
  108.1 2.4 %collective-permute-start.25 = (bf16[8,40,128]{2,1,0:T(8,128)(2,1)}, bf16[8,40,128]{2,1,0:T(8,128)(2,1)}, u32[]{:S(2)}, u32[]{:S(2)}) collective-permute-start(bf16[8,40,128]{2,1,0:T(8,128)(2,1)} %get-tuple-element.72), channel_id=1, source_target_pairs={{0,12},{4,0},{8,4},{12,8},{1,13},{5,1},{9,5},{13,9},{2,14},{6,2},{... | collective-permute-start | bytes 245768 | tf_op jit(solution)/shard_map/ppermute | solution.py:21
  110.5 1.8 %fusion.1 = bf16[64,2560]{1,0:T(8,128)(2,1)} fusion(f32[2,64,2560]{2,1,0:T(8,128)S(1)} %get-tuple-element.65, s32[]{:T(128)S(6)} %select_n.29, bf16[2,64,2560]{2,1,0:T(8,128)(2,1)} %collective-permute-done.21), kind=kLoop, calls=%fused_computation.3 | loop fusion | flops 491520 | bytes 1310724 | tf_op jit(solution)/shard_map/convert_element_type | solution.py:397
  112.2 2.6 %collective-permute-start.22 = (bf16[64,2560]{1,0:T(8,128)(2,1)}, bf16[64,2560]{1,0:T(8,128)(2,1)}, u32[]{:S(2)}, u32[]{:S(2)}) collective-permute-start(bf16[64,2560]{1,0:T(8,128)(2,1)} %fusion.1), channel_id=1, source_target_pairs={{0,2},{2,0},{1,3},{3,1},{4,6},{6,4},{5,7},{7,5},{8,10},{10,8},{9,1... | collective-permute-start | bytes 983048 | tf_op jit(solution)/shard_map/ppermute | solution.py:21
  116.5 1.7 %collective-permute-start.16 = (bf16[40,1024]{1,0:T(8,128)(2,1)S(1)}, bf16[40,1024]{1,0:T(8,128)(2,1)S(1)}, u32[]{:S(2)}, u32[]{:S(2)}) collective-permute-start(bf16[40,1024]{1,0:T(8,128)(2,1)S(1)} %dynamic-slice_bitcast_fusion), channel_id=1, source_target_pairs={{0,128},{128,0},{1,129},{129,1},{2,130},{130,2},{3,131},{131,3},{4... | collective-permute-start | bytes 245768 | tf_op jit(solution)/shard_map/ppermute | solution.py:21
  119.7 3.6 %all-to-all-start.3 = ((bf16[8,40,128]{2,1,0:T(8,128)(2,1)}), bf16[8,40,128]{2,1,0:T(8,128)(2,1)S(1)}, u32[]{:S(2)}, u32[]{:S(2)}) async-start(bf16[8,40,128]{2,1,0:T(8,128)(2,1)} %add_convert_fusion.1), calls=%async_computation.3 | async-start | bytes 163840 | tf_op jit(solution)/shard_map/all_to_all | solution.py:398
  123.3 2.4 %collective-permute-done.16 = bf16[40,1024]{1,0:T(8,128)(2,1)S(1)} collective-permute-done((bf16[40,1024]{1,0:T(8,128)(2,1)S(1)}, bf16[40,1024]{1,0:T(8,128)(2,1)S(1)}, u32[]{:S(2)}, u32[]{:S(2)}) %collective-permute-start.16) | collective-permute-done | bytes 81952 | tf_op jit(solution)/shard_map/ppermute | solution.py:21
  125.7 4.5 %shard_map.132 = (bf16[256,1024]{1,0:T(8,128)(2,1)}, bf16[256,128]{1,0:T(8,128)(2,1)}) custom-call(bf16[256,1024]{1,0:T(8,128)(2,1)S(1)} %bitcast.39, bf16[256,128]{1,0:T(8,128)(2,1)S(1)} %bitcast.47, bf16[256,128]{1,0:T(8,128)(2,1)S(1)} %bitcast.48, bf16[256,1024]{1,0:T(8,128)(2,1)S(1)} %bitcast.44, bf16[256,1024]{1,0:T(8,128)(2,1)S(1)} %get-tuple-element.60.grad_ref), custom_call_target="tpu_custom_call" | custom-call | flops 1 | bytes 1 | tf_op jit(solution)/shard_map/pallas_call | solution.py:233
  130.2 1.9 %fusion.2 = bf16[1,64,2560]{2,1,0:T(8,128)(2,1)} fusion(bf16[64,2560]{1,0:T(8,128)(2,1)} %collective-permute-done.22, f32[2,64,2560]{2,1,0:T(8,128)S(1)} %get-tuple-element.65, s32[]{:T(128)S(6)} %select_n.28, bf16[2,64,2560]{2,1,0:T(8,128)(2,1)} %collective-permute-done.21), kind=kLoop, calls=%fused_computation.4 | loop fusion | flops 819200 | bytes 1638404 | tf_op jit(solution)/shard_map/broadcast_in_dim | solution.py:413
  (78 shorter events, 21.1 us)
Async XLA Ops:
  1.5 4.8 %collective-permute-start = (bf16[40,1152]{1,0:T(8,128)(2,1)S(1)}, bf16[40,1152]{1,0:T(8,128)(2,1)S(1)}, u32[]{:S(2)}, u32[]{:S(2)}) collective-permute-start(bf16[40,1152]{1,0:T(8,128)(2,1)S(1)} %pad_maximum_fusion), channel_id=1, source_target_pairs={{0,128},{128,0},{1,129},{129,1},{2,130},{130,2},{3,131},{131,3},{4... | collective-permute-start | bytes 276488 | tf_op jit(solution)/shard_map/ppermute | solution.py:21
  5.5 16.7 %copy-start.6 = (bf16[1,64,2560]{2,1,0:T(8,128)(2,1)S(1)}, bf16[1,64,2560]{2,1,0:T(8,128)(2,1)}, u32[]{:S(2)}) copy-start(bf16[1,64,2560]{2,1,0:T(8,128)(2,1)} %param.12) | copy-start | bytes 983044
  7.4 21.6 %all-to-all-start = ((bf16[8,64,640]{2,1,0:T(8,128)(2,1)}), bf16[8,64,640]{2,1,0:T(8,128)(2,1)S(1)}, u32[]{:S(2)}, u32[]{:S(2)}) async-start(bf16[8,64,640]{2,1,0:T(8,128)(2,1)} %bitcast.11), calls=%async_computation | async-start | bytes 1310720 | tf_op jit(solution)/shard_map/all_to_all | solution.py:366
  13.1 30.5 %collective-permute-start.6 = (bf16[256,1024]{1,0:T(8,128)(2,1)S(1)}, bf16[256,1024]{1,0:T(8,128)(2,1)S(1)}, u32[]{:S(2)}, u32[]{:S(2)}) collective-permute-start(bf16[256,1024]{1,0:T(8,128)(2,1)S(1)} %bitcast.40), channel_id=1, source_target_pairs={{0,12},{4,0},{8,4},{12,8},{1,13},{5,1},{9,5},{13,9},{2,14},{6,2},{... | collective-permute-start | bytes 1572872 | tf_op jit(solution)/shard_map/ppermute | solution.py:21
  16.4 28.1 %collective-permute-start.5 = (bf16[256,1024]{1,0:T(8,128)(2,1)S(1)}, bf16[256,1024]{1,0:T(8,128)(2,1)S(1)}, u32[]{:S(2)}, u32[]{:S(2)}) collective-permute-start(bf16[256,1024]{1,0:T(8,128)(2,1)S(1)} %bitcast.41), channel_id=1, source_target_pairs={{0,4},{4,8},{8,12},{12,0},{1,5},{5,9},{9,13},{13,1},{2,6},{6,10},{... | collective-permute-start | bytes 1572872 | tf_op jit(solution)/shard_map/ppermute | solution.py:21
  16.4 8.9 %collective-permute-start.2 = (bf16[80,1152]{1,0:T(8,128)(2,1)S(1)}, bf16[80,1152]{1,0:T(8,128)(2,1)S(1)}, u32[]{:S(2)}, u32[]{:S(2)}) collective-permute-start(bf16[80,1152]{1,0:T(8,128)(2,1)S(1)} %maximum_select_fusion.refs_0_.refs_8_), channel_id=1, source_target_pairs={{0,112},{16,0},{32,16},{48,32},{64,48},{80,64},{96,80},{112,96},{1... | collective-permute-start | bytes 552968 | tf_op jit(solution)/shard_map/ppermute | solution.py:21
  22.2 6.7 %collective-permute-start.1 = (bf16[80,1152]{1,0:T(8,128)(2,1)S(1)}, bf16[80,1152]{1,0:T(8,128)(2,1)S(1)}, u32[]{:S(2)}, u32[]{:S(2)}) collective-permute-start(bf16[80,1152]{1,0:T(8,128)(2,1)S(1)} %maximum_select_fusion.refs_0_.refs_8_), channel_id=1, source_target_pairs={{0,16},{16,32},{32,48},{48,64},{64,80},{80,96},{96,112},{112,0},{1... | collective-permute-start | bytes 552968 | tf_op jit(solution)/shard_map/ppermute | solution.py:21
  29.0 23.0 %all-to-all-start.1 = ((bf16[4,64,1280]{2,1,0:T(8,128)(2,1)}), bf16[4,64,1280]{2,1,0:T(8,128)(2,1)}, u32[]{:S(2)}, u32[]{:S(2)}) async-start(bf16[4,64,1280]{2,1,0:T(8,128)(2,1)} %shard_map.127), calls=%async_computation.1 | async-start | bytes 1310720 | tf_op jit(solution)/shard_map/all_to_all | solution.py:370
  34.7 5.5 %collective-permute-start.4 = (bf16[80,1152]{1,0:T(8,128)(2,1)S(1)}, bf16[80,1152]{1,0:T(8,128)(2,1)S(1)}, u32[]{:S(2)}, u32[]{:S(2)}) collective-permute-start(bf16[80,1152]{1,0:T(8,128)(2,1)S(1)} %collective-permute-done.2.refs_2_.refs_10_), channel_id=1, source_target_pairs={{0,112},{16,0},{32,16},{48,32},{64,48},{80,64},{96,80},{112,96},{1... | collective-permute-start | bytes 552968 | tf_op jit(solution)/shard_map/ppermute | solution.py:21
  36.9 6.7 %collective-permute-start.3 = (bf16[80,1152]{1,0:T(8,128)(2,1)S(1)}, bf16[80,1152]{1,0:T(8,128)(2,1)S(1)}, u32[]{:S(2)}, u32[]{:S(2)}) collective-permute-start(bf16[80,1152]{1,0:T(8,128)(2,1)S(1)} %collective-permute-done.1.refs_1_.refs_9_), channel_id=1, source_target_pairs={{0,16},{16,32},{32,48},{48,64},{64,80},{80,96},{96,112},{112,0},{1... | collective-permute-start | bytes 552968 | tf_op jit(solution)/shard_map/ppermute | solution.py:21
  45.3 6.7 %collective-permute-start.7 = (bf16[80,1152]{1,0:T(8,128)(2,1)S(1)}, bf16[80,1152]{1,0:T(8,128)(2,1)S(1)}, u32[]{:S(2)}, u32[]{:S(2)}) collective-permute-start(bf16[80,1152]{1,0:T(8,128)(2,1)S(1)} %collective-permute-done.3.refs_3_.refs_11_), channel_id=1, source_target_pairs={{0,16},{16,32},{32,48},{48,64},{64,80},{80,96},{96,112},{112,0},{1... | collective-permute-start | bytes 552968 | tf_op jit(solution)/shard_map/ppermute | solution.py:21
  45.3 6.7 %collective-permute-start.8 = (bf16[80,1152]{1,0:T(8,128)(2,1)S(1)}, bf16[80,1152]{1,0:T(8,128)(2,1)S(1)}, u32[]{:S(2)}, u32[]{:S(2)}) collective-permute-start(bf16[80,1152]{1,0:T(8,128)(2,1)S(1)} %collective-permute-done.4.refs_4_.refs_12_), channel_id=1, source_target_pairs={{0,112},{16,0},{32,16},{48,32},{64,48},{80,64},{96,80},{112,96},{1... | collective-permute-start | bytes 552968 | tf_op jit(solution)/shard_map/ppermute | solution.py:21
  48.5 10.8 %collective-permute-start.11 = (bf16[256,1024]{1,0:T(8,128)(2,1)S(1)}, bf16[256,1024]{1,0:T(8,128)(2,1)}, u32[]{:S(2)}, u32[]{:S(2)}) collective-permute-start(bf16[256,1024]{1,0:T(8,128)(2,1)S(1)} %bitcast.42), channel_id=1, source_target_pairs={{0,8},{4,12},{8,0},{12,4},{1,9},{5,13},{9,1},{13,5},{2,10},{6,14},... | collective-permute-start | bytes 1572872 | tf_op jit(solution)/shard_map/ppermute | solution.py:21
  52.0 7.4 %collective-permute-start.9 = (bf16[4,64,1280]{2,1,0:T(8,128)(2,1)}, bf16[4,64,1280]{2,1,0:T(8,128)(2,1)}, u32[]{:S(2)}, u32[]{:S(2)}) collective-permute-start(bf16[4,64,1280]{2,1,0:T(8,128)(2,1)} %all-to-all-done.1.near_ref), channel_id=1, source_target_pairs={{0,1},{1,0},{2,3},{3,2},{4,5},{5,4},{6,7},{7,6},{8,9},{9,8},{10,11... | collective-permute-start | bytes 1966088 | tf_op jit(solution)/shard_map/ppermute | solution.py:21
  52.0 14.0 %collective-permute-start.10 = (bf16[8,64,640]{2,1,0:T(8,128)(2,1)S(1)}, bf16[8,64,640]{2,1,0:T(8,128)(2,1)S(1)}, u32[]{:S(2)}, u32[]{:S(2)}) collective-permute-start(bf16[8,64,640]{2,1,0:T(8,128)(2,1)S(1)} %all-to-all-done.near_ref), channel_id=1, source_target_pairs={{0,1},{1,0},{2,3},{3,2},{4,5},{5,4},{6,7},{7,6},{8,9},{9,8},{10,11... | collective-permute-start | bytes 1966088 | tf_op jit(solution)/shard_map/ppermute | solution.py:21
  59.3 6.7 %collective-permute-start.12 = (bf16[80,1152]{1,0:T(8,128)(2,1)S(1)}, bf16[80,1152]{1,0:T(8,128)(2,1)S(1)}, u32[]{:S(2)}, u32[]{:S(2)}) collective-permute-start(bf16[80,1152]{1,0:T(8,128)(2,1)S(1)} %collective-permute-done.7.refs_5_.refs_13_), channel_id=1, source_target_pairs={{0,16},{16,32},{32,48},{48,64},{64,80},{80,96},{96,112},{112,0},{1... | collective-permute-start | bytes 552968 | tf_op jit(solution)/shard_map/ppermute | solution.py:21
  59.4 16.0 %copy-start.5 = (bf16[256,1024]{1,0:T(8,128)(2,1)S(1)}, bf16[256,1024]{1,0:T(8,128)(2,1)}, u32[]{:S(2)}) copy-start(bf16[256,1024]{1,0:T(8,128)(2,1)} %copy-done.4) | copy-start | bytes 1572868
  71.3 15.4 %collective-permute-start.14 = (bf16[256,1024]{1,0:T(8,128)(2,1)}, bf16[256,1024]{1,0:T(8,128)(2,1)}, u32[]{:S(2)}, u32[]{:S(2)}) collective-permute-start(bf16[256,1024]{1,0:T(8,128)(2,1)} %get-tuple-element.51), channel_id=1, source_target_pairs={{0,8},{4,12},{8,0},{12,4},{1,9},{5,13},{9,1},{13,5},{2,10},{6,14},... | collective-permute-start | bytes 1572872 | tf_op jit(solution)/shard_map/ppermute | solution.py:21
  71.8 19.2 %collective-permute-start.15 = (bf16[256,1024]{1,0:T(8,128)(2,1)}, bf16[256,1024]{1,0:T(8,128)(2,1)}, u32[]{:S(2)}, u32[]{:S(2)}) collective-permute-start(bf16[256,1024]{1,0:T(8,128)(2,1)} %get-tuple-element.52), channel_id=1, source_target_pairs={{0,4},{4,8},{8,12},{12,0},{1,5},{5,9},{9,13},{13,1},{2,6},{6,10},{... | collective-permute-start | bytes 1572872 | tf_op jit(solution)/shard_map/ppermute | solution.py:21
  73.3 17.6 %collective-permute-start.13 = (bf16[256,1024]{1,0:T(8,128)(2,1)}, bf16[256,1024]{1,0:T(8,128)(2,1)}, u32[]{:S(2)}, u32[]{:S(2)}) collective-permute-start(bf16[256,1024]{1,0:T(8,128)(2,1)} %get-tuple-element.49), channel_id=1, source_target_pairs={{0,12},{4,0},{8,4},{12,8},{1,13},{5,1},{9,5},{13,9},{2,14},{6,2},{... | collective-permute-start | bytes 1572872 | tf_op jit(solution)/shard_map/ppermute | solution.py:21
  80.7 34.2 %all-to-all-start.2 = ((bf16[8,80,1024]{2,1,0:T(8,128)(2,1)}), bf16[8,80,1024]{2,1,0:T(8,128)(2,1)}, u32[]{:S(2)}, u32[]{:S(2)}) async-start(bf16[8,80,1024]{2,1,0:T(8,128)(2,1)} %bitcast.14), calls=%async_computation.2 | async-start | bytes 2621440 | tf_op jit(solution)/shard_map/all_to_all | solution.py:379
  93.5 4.5 %collective-permute-start.20 = (bf16[256,128]{1,0:T(8,128)(2,1)}, bf16[256,128]{1,0:T(8,128)(2,1)S(1)}, u32[]{:S(2)}, u32[]{:S(2)}) collective-permute-start(bf16[256,128]{1,0:T(8,128)(2,1)} %get-tuple-element.63.refs_0_), channel_id=1, source_target_pairs={{0,128},{128,0},{1,129},{129,1},{2,130},{130,2},{3,131},{131,3},{4... | collective-permute-start | bytes 196616 | tf_op jit(solution)/shard_map/ppermute | solution.py:21
  93.6 8.5 %collective-permute-start.19 = (bf16[640,128]{1,0:T(8,128)(2,1)S(1)}, bf16[640,128]{1,0:T(8,128)(2,1)S(1)}, u32[]{:S(2)}, u32[]{:S(2)}) collective-permute-start(bf16[640,128]{1,0:T(8,128)(2,1)S(1)} %get-tuple-element.64.refs_0_), channel_id=1, source_target_pairs={{0,12},{4,0},{8,4},{12,8},{1,13},{5,1},{9,5},{13,9},{2,14},{6,2},{... | collective-permute-start | bytes 491528 | tf_op jit(solution)/shard_map/ppermute | solution.py:21
  94.8 7.3 %collective-permute-start.18 = (bf16[640,128]{1,0:T(8,128)(2,1)S(1)}, bf16[640,128]{1,0:T(8,128)(2,1)S(1)}, u32[]{:S(2)}, u32[]{:S(2)}) collective-permute-start(bf16[640,128]{1,0:T(8,128)(2,1)S(1)} %get-tuple-element.64.refs_0_), channel_id=1, source_target_pairs={{0,8},{4,12},{8,0},{12,4},{1,9},{5,13},{9,1},{13,5},{2,10},{6,14},... | collective-permute-start | bytes 491528 | tf_op jit(solution)/shard_map/ppermute | solution.py:21
  96.8 6.6 %collective-permute-start.17 = (bf16[640,128]{1,0:T(8,128)(2,1)S(1)}, bf16[640,128]{1,0:T(8,128)(2,1)S(1)}, u32[]{:S(2)}, u32[]{:S(2)}) collective-permute-start(bf16[640,128]{1,0:T(8,128)(2,1)S(1)} %get-tuple-element.64.refs_0_), channel_id=1, source_target_pairs={{0,4},{4,8},{8,12},{12,0},{1,5},{5,9},{9,13},{13,1},{2,6},{6,10},{... | collective-permute-start | bytes 491528 | tf_op jit(solution)/shard_map/ppermute | solution.py:21
  105.8 4.6 %collective-permute-start.21 = (bf16[2,64,2560]{2,1,0:T(8,128)(2,1)}, bf16[2,64,2560]{2,1,0:T(8,128)(2,1)}, u32[]{:S(2)}, u32[]{:S(2)}) collective-permute-start(bf16[2,64,2560]{2,1,0:T(8,128)(2,1)} %get-tuple-element.68), channel_id=1, source_target_pairs={{0,1},{1,0},{2,3},{3,2},{4,5},{5,4},{6,7},{7,6},{8,9},{9,8},{10,11... | collective-permute-start | bytes 1966088 | tf_op jit(solution)/shard_map/ppermute | solution.py:21
  105.8 12.3 %collective-permute-start.23 = (bf16[8,40,128]{2,1,0:T(8,128)(2,1)}, bf16[8,40,128]{2,1,0:T(8,128)(2,1)S(1)}, u32[]{:S(2)}, u32[]{:S(2)}) collective-permute-start(bf16[8,40,128]{2,1,0:T(8,128)(2,1)} %get-tuple-element.70), channel_id=1, source_target_pairs={{0,4},{4,8},{8,12},{12,0},{1,5},{5,9},{9,13},{13,1},{2,6},{6,10},{... | collective-permute-start | bytes 245768 | tf_op jit(solution)/shard_map/ppermute | solution.py:21
  106.4 11.8 %collective-permute-start.24 = (bf16[8,40,128]{2,1,0:T(8,128)(2,1)}, bf16[8,40,128]{2,1,0:T(8,128)(2,1)}, u32[]{:S(2)}, u32[]{:S(2)}) collective-permute-start(bf16[8,40,128]{2,1,0:T(8,128)(2,1)} %get-tuple-element.71), channel_id=1, source_target_pairs={{0,8},{4,12},{8,0},{12,4},{1,9},{5,13},{9,1},{13,5},{2,10},{6,14},... | collective-permute-start | bytes 245768 | tf_op jit(solution)/shard_map/ppermute | solution.py:21
  108.1 10.1 %collective-permute-start.25 = (bf16[8,40,128]{2,1,0:T(8,128)(2,1)}, bf16[8,40,128]{2,1,0:T(8,128)(2,1)}, u32[]{:S(2)}, u32[]{:S(2)}) collective-permute-start(bf16[8,40,128]{2,1,0:T(8,128)(2,1)} %get-tuple-element.72), channel_id=1, source_target_pairs={{0,12},{4,0},{8,4},{12,8},{1,13},{5,1},{9,5},{13,9},{2,14},{6,2},{... | collective-permute-start | bytes 245768 | tf_op jit(solution)/shard_map/ppermute | solution.py:21
  112.2 18.0 %collective-permute-start.22 = (bf16[64,2560]{1,0:T(8,128)(2,1)}, bf16[64,2560]{1,0:T(8,128)(2,1)}, u32[]{:S(2)}, u32[]{:S(2)}) collective-permute-start(bf16[64,2560]{1,0:T(8,128)(2,1)} %fusion.1), channel_id=1, source_target_pairs={{0,2},{2,0},{1,3},{3,1},{4,6},{6,4},{5,7},{7,5},{8,10},{10,8},{9,1... | collective-permute-start | bytes 983048 | tf_op jit(solution)/shard_map/ppermute | solution.py:21
  116.5 9.2 %collective-permute-start.16 = (bf16[40,1024]{1,0:T(8,128)(2,1)S(1)}, bf16[40,1024]{1,0:T(8,128)(2,1)S(1)}, u32[]{:S(2)}, u32[]{:S(2)}) collective-permute-start(bf16[40,1024]{1,0:T(8,128)(2,1)S(1)} %dynamic-slice_bitcast_fusion), channel_id=1, source_target_pairs={{0,128},{128,0},{1,129},{129,1},{2,130},{130,2},{3,131},{131,3},{4... | collective-permute-start | bytes 245768 | tf_op jit(solution)/shard_map/ppermute | solution.py:21
  119.7 13.0 %all-to-all-start.3 = ((bf16[8,40,128]{2,1,0:T(8,128)(2,1)}), bf16[8,40,128]{2,1,0:T(8,128)(2,1)S(1)}, u32[]{:S(2)}, u32[]{:S(2)}) async-start(bf16[8,40,128]{2,1,0:T(8,128)(2,1)} %add_convert_fusion.1), calls=%async_computation.3 | async-start | bytes 163840 | tf_op jit(solution)/shard_map/all_to_all | solution.py:398
  (12 other events, 66.1 us)
where the time goes:
time: 134 us; the launch traced here: 133 us
  starting transfers between devices  53.6 us (40%)
  waiting for transfers between devices  39.1 us (29%)
  Pallas kernels  25.7 us (19%)
  other arithmetic  9.13 us (7%)
  local copies, waits for them, and re-layouts  5.05 us (4%)
    ppermute x26, waiting for transfers between devices, shift(): lax.ppermute(array, axis, [(i, (i + by) % count) for i in range(count)])  39.1 us
    ppermute x26, starting transfers between devices, shift(): lax.ppermute(array, axis, [(i, (i + by) % count) for i in range(count)])  34.1 us
    all_to_all x1, starting transfers between devices, on_device(): lax.all_to_all(after(for_each(by_y), plane), ('y', 'xh'), 0, 0, tiled=True)  5.78 us
    all_to_all x1, starting transfers between devices, on_device(): lax.all_to_all(after(split(li, n_xl), near), ('xl', 'xh'), 0, 0, tiled=True)  5.67 us
    pallas_call x1, Pallas kernels, out_part(): pl.pallas_call(out_kernel, grid_spec=pltpu.PrefetchScalarGridSpec(num_sca...  5.32 us
    pallas_call x1, Pallas kernels, head_parts(): pl.pallas_call(functools.partial(head_kernel, tuple(pieces)), grid_spec=p...  5.27 us
    pallas_call x1, Pallas kernels, score_gradients(): pl.pallas_call(functools.partial(score_kernel, HEAD ** (-0.5), heads), gr...  4.5 us
    all_to_all x1, starting transfers between devices, on_device(): lax.all_to_all(part.reshape(n_z, n_xl * cols, width), 'z', 0, 0, tiled=True)  4.41 us
  transfers between devices with their start and end apart: 30, of which 12 were waited for; matrix products, arithmetic and copies ran while one was open for 7% of the time, Pallas kernels for 15%

commit v1 on v0

--- a/solution.py
+++ b/solution.py
@@ -145,7 +145,7 @@
 def head_parts(place, near, far, pieces, seq, width):
     feats = near.shape[2]
     count = near.shape[0] // 2
-    block = 256
+    block = 512
     depth = feats // len(pieces)
     wide = pl.BlockSpec((seq, block), lambda i, place: (0, i))
     return pl.pallas_call(
@@ -226,7 +226,7 @@
 
 def score_gradients(q, k, v, ao, grad):
     seq, width = q.shape
-    heads = 2
+    heads = 4
     count = width // HEAD
     wide = pl.BlockSpec((seq, heads * HEAD), lambda i: (0, i))
     narrow = whole((seq, HEAD))

time: 134 us -> 133 us (level)
  no operation moved by 1% of the time
where the time goes in v1:
time: 133 us; the launch traced here: 132 us
  starting transfers between devices  53.6 us (40%)
  waiting for transfers between devices  39.1 us (29%)
  Pallas kernels  24.8 us (19%)
  other arithmetic  9.13 us (7%)
  local copies, waits for them, and re-layouts  5.05 us (4%)
    ppermute x26, waiting for transfers between devices, shift(): lax.ppermute(array, axis, [(i, (i + by) % count) for i in range(count)])  39.1 us
    ppermute x26, starting transfers between devices, shift(): lax.ppermute(array, axis, [(i, (i + by) % count) for i in range(count)])  34.2 us
    all_to_all x1, starting transfers between devices, on_device(): lax.all_to_all(after(for_each(by_y), plane), ('y', 'xh'), 0, 0, tiled=True)  5.78 us
    all_to_all x1, starting transfers between devices, on_device(): lax.all_to_all(after(split(li, n_xl), near), ('xl', 'xh'), 0, 0, tiled=True)  5.67 us
    pallas_call x1, Pallas kernels, out_part(): pl.pallas_call(out_kernel, grid_spec=pltpu.PrefetchScalarGridSpec(num_sca...  5.31 us
    pallas_call x1, Pallas kernels, head_parts(): pl.pallas_call(functools.partial(head_kernel, tuple(pieces)), grid_spec=p...  4.48 us
    all_to_all x1, starting transfers between devices, on_device(): lax.all_to_all(part.reshape(n_z, n_xl * cols, width), 'z', 0, 0, tiled=True)  4.41 us
    pallas_call x1, Pallas kernels, score_gradients(): pl.pallas_call(functools.partial(score_kernel, HEAD ** (-0.5), heads), gr...  4.36 us
  transfers between devices with their start and end apart: 30, of which 12 were waited for; matrix products, arithmetic and copies ran while one was open for 7% of the time, Pallas kernels for 15%

profile of v1, /device:TPU:2, one launch (start us, length us, event | category | flops | bytes accessed | tf_op | source)
XLA Modules:
  0.0 132.5 jit_solution(2080600185627721863)
XLA Ops:
  1.5 2.3 %collective-permute-start = (bf16[40,1152]{1,0:T(8,128)(2,1)S(1)}, bf16[40,1152]{1,0:T(8,128)(2,1)S(1)}, u32[]{:S(2)}, u32[]{:S(2)}) collective-permute-start(bf16[40,1152]{1,0:T(8,128)(2,1)S(1)} %pad_maximum_fusion), channel_id=1, source_target_pairs={{0,128},{128,0},{1,129},{129,1},{2,130},{130,2},{3,131},{131,3},{4... | collective-permute-start | bytes 276488 | tf_op jit(solution)/shard_map/ppermute | solution.py:21
  7.4 5.8 %all-to-all-start = ((bf16[8,64,640]{2,1,0:T(8,128)(2,1)}), bf16[8,64,640]{2,1,0:T(8,128)(2,1)S(1)}, u32[]{:S(2)}, u32[]{:S(2)}) async-start(bf16[8,64,640]{2,1,0:T(8,128)(2,1)} %bitcast.11), calls=%async_computation | async-start | bytes 1310720 | tf_op jit(solution)/shard_map/all_to_all | solution.py:366
  13.1 3.2 %collective-permute-start.6 = (bf16[256,1024]{1,0:T(8,128)(2,1)S(1)}, bf16[256,1024]{1,0:T(8,128)(2,1)S(1)}, u32[]{:S(2)}, u32[]{:S(2)}) collective-permute-start(bf16[256,1024]{1,0:T(8,128)(2,1)S(1)} %bitcast.40), channel_id=1, source_target_pairs={{0,12},{4,0},{8,4},{12,8},{1,13},{5,1},{9,5},{13,9},{2,14},{6,2},{... | collective-permute-start | bytes 1572872 | tf_op jit(solution)/shard_map/ppermute | solution.py:21
  16.4 5.9 %collective-permute-start.2 = (bf16[80,1152]{1,0:T(8,128)(2,1)S(1)}, bf16[80,1152]{1,0:T(8,128)(2,1)S(1)}, u32[]{:S(2)}, u32[]{:S(2)}) collective-permute-start(bf16[80,1152]{1,0:T(8,128)(2,1)S(1)} %maximum_select_fusion.refs_0_.refs_8_), channel_id=1, source_target_pairs={{0,112},{16,0},{32,16},{48,32},{64,48},{80,64},{96,80},{112,96},{1... | collective-permute-start | bytes 552968 | tf_op jit(solution)/shard_map/ppermute | solution.py:21
  23.1 2.2 %collective-permute-done.2.refs_2_.refs_10_ = bf16[80,1152]{1,0:T(8,128)(2,1)S(1)} collective-permute-done((bf16[80,1152]{1,0:T(8,128)(2,1)S(1)}, bf16[80,1152]{1,0:T(8,128)(2,1)S(1)}, u32[]{:S(2)}, u32[]{:S(2)}) %collective-permute-start.2) | collective-permute-done | bytes 184352 | tf_op jit(solution)/shard_map/ppermute | solution.py:21
  25.3 3.7 %collective-permute-done.1.refs_1_.refs_9_ = bf16[80,1152]{1,0:T(8,128)(2,1)S(1)} collective-permute-done((bf16[80,1152]{1,0:T(8,128)(2,1)S(1)}, bf16[80,1152]{1,0:T(8,128)(2,1)S(1)}, u32[]{:S(2)}, u32[]{:S(2)}) %collective-permute-start.1) | collective-permute-done | bytes 184352 | tf_op jit(solution)/shard_map/ppermute | solution.py:21
  29.0 5.7 %all-to-all-start.1 = ((bf16[4,64,1280]{2,1,0:T(8,128)(2,1)}), bf16[4,64,1280]{2,1,0:T(8,128)(2,1)}, u32[]{:S(2)}, u32[]{:S(2)}) async-start(bf16[4,64,1280]{2,1,0:T(8,128)(2,1)} %shard_map.127), calls=%async_computation.1 | async-start | bytes 1310720 | tf_op jit(solution)/shard_map/all_to_all | solution.py:370
  34.7 2.2 %collective-permute-start.4 = (bf16[80,1152]{1,0:T(8,128)(2,1)S(1)}, bf16[80,1152]{1,0:T(8,128)(2,1)S(1)}, u32[]{:S(2)}, u32[]{:S(2)}) collective-permute-start(bf16[80,1152]{1,0:T(8,128)(2,1)S(1)} %collective-permute-done.2.refs_2_.refs_10_), channel_id=1, source_target_pairs={{0,112},{16,0},{32,16},{48,32},{64,48},{80,64},{96,80},{112,96},{1... | collective-permute-start | bytes 552968 | tf_op jit(solution)/shard_map/ppermute | solution.py:21
  36.9 3.3 %collective-permute-done.4.refs_4_.refs_12_ = bf16[80,1152]{1,0:T(8,128)(2,1)S(1)} collective-permute-done((bf16[80,1152]{1,0:T(8,128)(2,1)S(1)}, bf16[80,1152]{1,0:T(8,128)(2,1)S(1)}, u32[]{:S(2)}, u32[]{:S(2)}) %collective-permute-start.4) | collective-permute-done | bytes 184352 | tf_op jit(solution)/shard_map/ppermute | solution.py:21
  40.2 3.5 %collective-permute-done.3.refs_3_.refs_11_ = bf16[80,1152]{1,0:T(8,128)(2,1)S(1)} collective-permute-done((bf16[80,1152]{1,0:T(8,128)(2,1)S(1)}, bf16[80,1152]{1,0:T(8,128)(2,1)S(1)}, u32[]{:S(2)}, u32[]{:S(2)}) %collective-permute-start.3) | collective-permute-done | bytes 184352 | tf_op jit(solution)/shard_map/ppermute | solution.py:21
  45.3 3.2 %collective-permute-start.8 = (bf16[80,1152]{1,0:T(8,128)(2,1)S(1)}, bf16[80,1152]{1,0:T(8,128)(2,1)S(1)}, u32[]{:S(2)}, u32[]{:S(2)}) collective-permute-start(bf16[80,1152]{1,0:T(8,128)(2,1)S(1)} %collective-permute-done.4.refs_4_.refs_12_), channel_id=1, source_target_pairs={{0,112},{16,0},{32,16},{48,32},{64,48},{80,64},{96,80},{112,96},{1... | collective-permute-start | bytes 552968 | tf_op jit(solution)/shard_map/ppermute | solution.py:21
  49.0 3.1 %collective-permute-done.7.refs_5_.refs_13_ = bf16[80,1152]{1,0:T(8,128)(2,1)S(1)} collective-permute-done((bf16[80,1152]{1,0:T(8,128)(2,1)S(1)}, bf16[80,1152]{1,0:T(8,128)(2,1)S(1)}, u32[]{:S(2)}, u32[]{:S(2)}) %collective-permute-start.7) | collective-permute-done | bytes 184352 | tf_op jit(solution)/shard_map/ppermute | solution.py:21
  52.5 6.8 %collective-permute-done.11.refs_2_ = bf16[256,1024]{1,0:T(8,128)(2,1)} collective-permute-done((bf16[256,1024]{1,0:T(8,128)(2,1)S(1)}, bf16[256,1024]{1,0:T(8,128)(2,1)}, u32[]{:S(2)}, u32[]{:S(2)}) %collective-permute-start.11) | collective-permute-done | bytes 524320 | tf_op jit(solution)/shard_map/ppermute | solution.py:21
  59.4 6.7 %collective-permute-done.12.refs_7_.refs_15_ = bf16[80,1152]{1,0:T(8,128)(2,1)S(1)} collective-permute-done((bf16[80,1152]{1,0:T(8,128)(2,1)S(1)}, bf16[80,1152]{1,0:T(8,128)(2,1)S(1)}, u32[]{:S(2)}, u32[]{:S(2)}) %collective-permute-start.12) | collective-permute-done | bytes 184352 | tf_op jit(solution)/shard_map/ppermute | solution.py:21
  66.1 4.5 %shard_map.128 = (f32[256,1024]{1,0:T(8,128)S(1)}, bf16[256,1024]{1,0:T(8,128)(2,1)}, bf16[256,1024]{1,0:T(8,128)(2,1)}, bf16[256,1024]{1,0:T(8,128)(2,1)}, bf16[640,128]{1,0:T(8,128)(2,1)S(1)}) custom-call(s32[4]{0:T(128)S(1)} %pad_add_fusion.place, bf16[8,64,640]{2,1,0:T(8,128)(2,1)S(1)} %all-to-all-done.near_ref, ...), custom_call_target="tpu_custom_call" | custom-call | flops 1 | bytes 1 | tf_op jit(solution)/shard_map/pallas_call | solution.py:151
  72.6 2.0 %collective-permute-start.13 = (bf16[256,1024]{1,0:T(8,128)(2,1)}, bf16[256,1024]{1,0:T(8,128)(2,1)}, u32[]{:S(2)}, u32[]{:S(2)}) collective-permute-start(bf16[256,1024]{1,0:T(8,128)(2,1)} %get-tuple-element.49), channel_id=1, source_target_pairs={{0,12},{4,0},{8,4},{12,8},{1,13},{5,1},{9,5},{13,9},{2,14},{6,2},{... | collective-permute-start | bytes 1572872 | tf_op jit(solution)/shard_map/ppermute | solution.py:21
  74.6 5.3 %shard_map.131 = bf16[640,1024]{1,0:T(8,128)(2,1)} custom-call(s32[4]{0:T(128)S(1)} %pad_add_fusion.place, bf16[8,64,640]{2,1,0:T(8,128)(2,1)S(1)} %all-to-all-done.near_ref, bf16[8,64,640]{2,1,0:T(8,128)(2,1)S(1)} %collective-permute-done.10.far_ref, bf16[256,1024]{1,0:T(8,128)(2,1)S(1)} %bitcast.43, bf16[256,1024]{1,0:T(8,128)(2,1)S(1)} %copy-done.5, ...), custom_call_target="tpu_custom_call" | custom-call | flops 1 | bytes 1 | tf_op jit(solution)/shard_map/pallas_call | solution.py:106
  79.9 4.4 %all-to-all-start.2 = ((bf16[8,80,1024]{2,1,0:T(8,128)(2,1)}), bf16[8,80,1024]{2,1,0:T(8,128)(2,1)}, u32[]{:S(2)}, u32[]{:S(2)}) async-start(bf16[8,80,1024]{2,1,0:T(8,128)(2,1)} %bitcast.14), calls=%async_computation.2 | async-start | bytes 2621440 | tf_op jit(solution)/shard_map/all_to_all | solution.py:379
  85.9 4.3 %collective-permute-done.15.refs_2_ = bf16[256,1024]{1,0:T(8,128)(2,1)} collective-permute-done((bf16[256,1024]{1,0:T(8,128)(2,1)}, bf16[256,1024]{1,0:T(8,128)(2,1)}, u32[]{:S(2)}, u32[]{:S(2)}) %collective-permute-start.15) | collective-permute-done | bytes 524320 | tf_op jit(solution)/shard_map/ppermute | solution.py:21
  90.2 2.5 %shard_map.130 = (bf16[256,1024]{1,0:T(8,128)(2,1)S(1)}, bf16[256,128]{1,0:T(8,128)(2,1)}) custom-call(bf16[8,256,256]{2,1,0:T(8,128)(2,1)S(1)} %shard_map.129.probs_ref, f32[256,1024]{1,0:T(8,128)S(1)} %copy-done.10, bf16[256,1024]{1,0:T(8,128)(2,1)} %collective-permute-done.13.refs_0_, bf16[256,1024]{1,0:T(8,128)(2,1)} %collective-permute-done.14.refs_1_, ...), custom_call_target="tpu_custom_call" | custom-call | flops 4000000000 | bytes 10000000 | tf_op jit(solution)/shard_map/pallas_call | solution.py:186
  94.0 2.0 %collective-permute-start.18 = (bf16[640,128]{1,0:T(8,128)(2,1)S(1)}, bf16[640,128]{1,0:T(8,128)(2,1)S(1)}, u32[]{:S(2)}, u32[]{:S(2)}) collective-permute-start(bf16[640,128]{1,0:T(8,128)(2,1)S(1)} %get-tuple-element.64.refs_0_), channel_id=1, source_target_pairs={{0,8},{4,12},{8,0},{12,4},{1,9},{5,13},{9,1},{13,5},{2,10},{6,14},... | collective-permute-start | bytes 491528 | tf_op jit(solution)/shard_map/ppermute | solution.py:21
  98.0 3.3 %shard_map.134 = (bf16[8,40,128]{2,1,0:T(8,128)(2,1)S(1)}, bf16[8,40,128]{2,1,0:T(8,128)(2,1)}, bf16[8,40,128]{2,1,0:T(8,128)(2,1)}, bf16[8,40,128]{2,1,0:T(8,128)(2,1)}) custom-call(s32[4]{0:T(128)S(1)} %pad_add_fusion.place, bf16[4,64,1280]{2,1,0:T(8,128)(2,1)} %all-to-all-done.1.near_ref, bf16[4,64,1280]{2,1,0:T(8,128)(2,1)} %collective-permute-done.9.far_ref, ...), custom_call_target="tpu_custom_call" | custom-call | flops 4000000000 | bytes 10000000 | tf_op jit(solution)/shard_map/pallas_call | solution.py:303
  102.5 2.5 %shard_map.133 = (f32[2,64,2560]{2,1,0:T(8,128)S(1)}, bf16[2,64,2560]{2,1,0:T(8,128)(2,1)}) custom-call(s32[4]{0:T(128)S(1)} %pad_add_fusion.place, bf16[2,2,64,128]{3,2,1,0:T(8,128)(2,1)S(1)} %bitcast.50, bf16[640,128]{1,0:T(8,128)(2,1)S(1)} %get-tuple-element.64.refs_0_, bf16[640,128]{1,0:T(8,128)(2,1)S(1)} %collective-permute-done.17.refs_1_, ...), custom_call_target="tpu_custom_call" | custom-call | flops 4000000000 | bytes 10000000 | tf_op jit(solution)/shard_map/pallas_call | solution.py:266
  105.6 1.7 %collective-permute-start.24 = (bf16[8,40,128]{2,1,0:T(8,128)(2,1)}, bf16[8,40,128]{2,1,0:T(8,128)(2,1)}, u32[]{:S(2)}, u32[]{:S(2)}) collective-permute-start(bf16[8,40,128]{2,1,0:T(8,128)(2,1)} %get-tuple-element.71), channel_id=1, source_target_pairs={{0,8},{4,12},{8,0},{12,4},{1,9},{5,13},{9,1},{13,5},{2,10},{6,14},... | collective-permute-start | bytes 245768 | tf_op jit(solution)/shard_map/ppermute | solution.py:21
  107.3 2.4 %collective-permute-start.25 = (bf16[8,40,128]{2,1,0:T(8,128)(2,1)}, bf16[8,40,128]{2,1,0:T(8,128)(2,1)}, u32[]{:S(2)}, u32[]{:S(2)}) collective-permute-start(bf16[8,40,128]{2,1,0:T(8,128)(2,1)} %get-tuple-element.72), channel_id=1, source_target_pairs={{0,12},{4,0},{8,4},{12,8},{1,13},{5,1},{9,5},{13,9},{2,14},{6,2},{... | collective-permute-start | bytes 245768 | tf_op jit(solution)/shard_map/ppermute | solution.py:21
  109.7 1.8 %fusion.1 = bf16[64,2560]{1,0:T(8,128)(2,1)} fusion(f32[2,64,2560]{2,1,0:T(8,128)S(1)} %get-tuple-element.65, s32[]{:T(128)S(6)} %select_n.29, bf16[2,64,2560]{2,1,0:T(8,128)(2,1)} %collective-permute-done.21), kind=kLoop, calls=%fused_computation.3 | loop fusion | flops 491520 | bytes 1310724 | tf_op jit(solution)/shard_map/convert_element_type | solution.py:397
  111.4 2.6 %collective-permute-start.22 = (bf16[64,2560]{1,0:T(8,128)(2,1)}, bf16[64,2560]{1,0:T(8,128)(2,1)}, u32[]{:S(2)}, u32[]{:S(2)}) collective-permute-start(bf16[64,2560]{1,0:T(8,128)(2,1)} %fusion.1), channel_id=1, source_target_pairs={{0,2},{2,0},{1,3},{3,1},{4,6},{6,4},{5,7},{7,5},{8,10},{10,8},{9,1... | collective-permute-start | bytes 983048 | tf_op jit(solution)/shard_map/ppermute | solution.py:21
  115.7 1.7 %collective-permute-start.16 = (bf16[40,1024]{1,0:T(8,128)(2,1)S(1)}, bf16[40,1024]{1,0:T(8,128)(2,1)S(1)}, u32[]{:S(2)}, u32[]{:S(2)}) collective-permute-start(bf16[40,1024]{1,0:T(8,128)(2,1)S(1)} %dynamic-slice_bitcast_fusion), channel_id=1, source_target_pairs={{0,128},{128,0},{1,129},{129,1},{2,130},{130,2},{3,131},{131,3},{4... | collective-permute-start | bytes 245768 | tf_op jit(solution)/shard_map/ppermute | solution.py:21
  119.0 3.6 %all-to-all-start.3 = ((bf16[8,40,128]{2,1,0:T(8,128)(2,1)}), bf16[8,40,128]{2,1,0:T(8,128)(2,1)S(1)}, u32[]{:S(2)}, u32[]{:S(2)}) async-start(bf16[8,40,128]{2,1,0:T(8,128)(2,1)} %add_convert_fusion.1), calls=%async_computation.3 | async-start | bytes 163840 | tf_op jit(solution)/shard_map/all_to_all | solution.py:398
  122.5 2.4 %collective-permute-done.16 = bf16[40,1024]{1,0:T(8,128)(2,1)S(1)} collective-permute-done((bf16[40,1024]{1,0:T(8,128)(2,1)S(1)}, bf16[40,1024]{1,0:T(8,128)(2,1)S(1)}, u32[]{:S(2)}, u32[]{:S(2)}) %collective-permute-start.16) | collective-permute-done | bytes 81952 | tf_op jit(solution)/shard_map/ppermute | solution.py:21
  124.9 4.4 %shard_map.132 = (bf16[256,1024]{1,0:T(8,128)(2,1)}, bf16[256,128]{1,0:T(8,128)(2,1)}) custom-call(bf16[256,1024]{1,0:T(8,128)(2,1)S(1)} %bitcast.39, bf16[256,128]{1,0:T(8,128)(2,1)S(1)} %bitcast.47, bf16[256,128]{1,0:T(8,128)(2,1)S(1)} %bitcast.48, bf16[256,1024]{1,0:T(8,128)(2,1)S(1)} %bitcast.44, bf16[256,1024]{1,0:T(8,128)(2,1)S(1)} %get-tuple-element.60.grad_ref), custom_call_target="tpu_custom_call" | custom-call | flops 1 | bytes 1 | tf_op jit(solution)/shard_map/pallas_call | solution.py:233
  129.3 1.9 %fusion.2 = bf16[1,64,2560]{2,1,0:T(8,128)(2,1)} fusion(bf16[64,2560]{1,0:T(8,128)(2,1)} %collective-permute-done.22, f32[2,64,2560]{2,1,0:T(8,128)S(1)} %get-tuple-element.65, s32[]{:T(128)S(6)} %select_n.28, bf16[2,64,2560]{2,1,0:T(8,128)(2,1)} %collective-permute-done.21), kind=kLoop, calls=%fused_computation.4 | loop fusion | flops 819200 | bytes 1638404 | tf_op jit(solution)/shard_map/broadcast_in_dim | solution.py:413
  (78 shorter events, 21.1 us)
Async XLA Ops:
  1.5 4.8 %collective-permute-start = (bf16[40,1152]{1,0:T(8,128)(2,1)S(1)}, bf16[40,1152]{1,0:T(8,128)(2,1)S(1)}, u32[]{:S(2)}, u32[]{:S(2)}) collective-permute-start(bf16[40,1152]{1,0:T(8,128)(2,1)S(1)} %pad_maximum_fusion), channel_id=1, source_target_pairs={{0,128},{128,0},{1,129},{129,1},{2,130},{130,2},{3,131},{131,3},{4... | collective-permute-start | bytes 276488 | tf_op jit(solution)/shard_map/ppermute | solution.py:21
  5.5 16.7 %copy-start.6 = (bf16[1,64,2560]{2,1,0:T(8,128)(2,1)S(1)}, bf16[1,64,2560]{2,1,0:T(8,128)(2,1)}, u32[]{:S(2)}) copy-start(bf16[1,64,2560]{2,1,0:T(8,128)(2,1)} %param.12) | copy-start | bytes 983044
  7.4 21.6 %all-to-all-start = ((bf16[8,64,640]{2,1,0:T(8,128)(2,1)}), bf16[8,64,640]{2,1,0:T(8,128)(2,1)S(1)}, u32[]{:S(2)}, u32[]{:S(2)}) async-start(bf16[8,64,640]{2,1,0:T(8,128)(2,1)} %bitcast.11), calls=%async_computation | async-start | bytes 1310720 | tf_op jit(solution)/shard_map/all_to_all | solution.py:366
  13.1 30.5 %collective-permute-start.6 = (bf16[256,1024]{1,0:T(8,128)(2,1)S(1)}, bf16[256,1024]{1,0:T(8,128)(2,1)S(1)}, u32[]{:S(2)}, u32[]{:S(2)}) collective-permute-start(bf16[256,1024]{1,0:T(8,128)(2,1)S(1)} %bitcast.40), channel_id=1, source_target_pairs={{0,12},{4,0},{8,4},{12,8},{1,13},{5,1},{9,5},{13,9},{2,14},{6,2},{... | collective-permute-start | bytes 1572872 | tf_op jit(solution)/shard_map/ppermute | solution.py:21
  16.4 28.1 %collective-permute-start.5 = (bf16[256,1024]{1,0:T(8,128)(2,1)S(1)}, bf16[256,1024]{1,0:T(8,128)(2,1)S(1)}, u32[]{:S(2)}, u32[]{:S(2)}) collective-permute-start(bf16[256,1024]{1,0:T(8,128)(2,1)S(1)} %bitcast.41), channel_id=1, source_target_pairs={{0,4},{4,8},{8,12},{12,0},{1,5},{5,9},{9,13},{13,1},{2,6},{6,10},{... | collective-permute-start | bytes 1572872 | tf_op jit(solution)/shard_map/ppermute | solution.py:21
  16.4 8.9 %collective-permute-start.2 = (bf16[80,1152]{1,0:T(8,128)(2,1)S(1)}, bf16[80,1152]{1,0:T(8,128)(2,1)S(1)}, u32[]{:S(2)}, u32[]{:S(2)}) collective-permute-start(bf16[80,1152]{1,0:T(8,128)(2,1)S(1)} %maximum_select_fusion.refs_0_.refs_8_), channel_id=1, source_target_pairs={{0,112},{16,0},{32,16},{48,32},{64,48},{80,64},{96,80},{112,96},{1... | collective-permute-start | bytes 552968 | tf_op jit(solution)/shard_map/ppermute | solution.py:21
  22.2 6.7 %collective-permute-start.1 = (bf16[80,1152]{1,0:T(8,128)(2,1)S(1)}, bf16[80,1152]{1,0:T(8,128)(2,1)S(1)}, u32[]{:S(2)}, u32[]{:S(2)}) collective-permute-start(bf16[80,1152]{1,0:T(8,128)(2,1)S(1)} %maximum_select_fusion.refs_0_.refs_8_), channel_id=1, source_target_pairs={{0,16},{16,32},{32,48},{48,64},{64,80},{80,96},{96,112},{112,0},{1... | collective-permute-start | bytes 552968 | tf_op jit(solution)/shard_map/ppermute | solution.py:21
  29.0 23.0 %all-to-all-start.1 = ((bf16[4,64,1280]{2,1,0:T(8,128)(2,1)}), bf16[4,64,1280]{2,1,0:T(8,128)(2,1)}, u32[]{:S(2)}, u32[]{:S(2)}) async-start(bf16[4,64,1280]{2,1,0:T(8,128)(2,1)} %shard_map.127), calls=%async_computation.1 | async-start | bytes 1310720 | tf_op jit(solution)/shard_map/all_to_all | solution.py:370
  34.7 5.5 %collective-permute-start.4 = (bf16[80,1152]{1,0:T(8,128)(2,1)S(1)}, bf16[80,1152]{1,0:T(8,128)(2,1)S(1)}, u32[]{:S(2)}, u32[]{:S(2)}) collective-permute-start(bf16[80,1152]{1,0:T(8,128)(2,1)S(1)} %collective-permute-done.2.refs_2_.refs_10_), channel_id=1, source_target_pairs={{0,112},{16,0},{32,16},{48,32},{64,48},{80,64},{96,80},{112,96},{1... | collective-permute-start | bytes 552968 | tf_op jit(solution)/shard_map/ppermute | solution.py:21
  36.9 6.7 %collective-permute-start.3 = (bf16[80,1152]{1,0:T(8,128)(2,1)S(1)}, bf16[80,1152]{1,0:T(8,128)(2,1)S(1)}, u32[]{:S(2)}, u32[]{:S(2)}) collective-permute-start(bf16[80,1152]{1,0:T(8,128)(2,1)S(1)} %collective-permute-done.1.refs_1_.refs_9_), channel_id=1, source_target_pairs={{0,16},{16,32},{32,48},{48,64},{64,80},{80,96},{96,112},{112,0},{1... | collective-permute-start | bytes 552968 | tf_op jit(solution)/shard_map/ppermute | solution.py:21
  45.3 6.7 %collective-permute-start.7 = (bf16[80,1152]{1,0:T(8,128)(2,1)S(1)}, bf16[80,1152]{1,0:T(8,128)(2,1)S(1)}, u32[]{:S(2)}, u32[]{:S(2)}) collective-permute-start(bf16[80,1152]{1,0:T(8,128)(2,1)S(1)} %collective-permute-done.3.refs_3_.refs_11_), channel_id=1, source_target_pairs={{0,16},{16,32},{32,48},{48,64},{64,80},{80,96},{96,112},{112,0},{1... | collective-permute-start | bytes 552968 | tf_op jit(solution)/shard_map/ppermute | solution.py:21
  45.3 6.7 %collective-permute-start.8 = (bf16[80,1152]{1,0:T(8,128)(2,1)S(1)}, bf16[80,1152]{1,0:T(8,128)(2,1)S(1)}, u32[]{:S(2)}, u32[]{:S(2)}) collective-permute-start(bf16[80,1152]{1,0:T(8,128)(2,1)S(1)} %collective-permute-done.4.refs_4_.refs_12_), channel_id=1, source_target_pairs={{0,112},{16,0},{32,16},{48,32},{64,48},{80,64},{96,80},{112,96},{1... | collective-permute-start | bytes 552968 | tf_op jit(solution)/shard_map/ppermute | solution.py:21
  48.5 10.8 %collective-permute-start.11 = (bf16[256,1024]{1,0:T(8,128)(2,1)S(1)}, bf16[256,1024]{1,0:T(8,128)(2,1)}, u32[]{:S(2)}, u32[]{:S(2)}) collective-permute-start(bf16[256,1024]{1,0:T(8,128)(2,1)S(1)} %bitcast.42), channel_id=1, source_target_pairs={{0,8},{4,12},{8,0},{12,4},{1,9},{5,13},{9,1},{13,5},{2,10},{6,14},... | collective-permute-start | bytes 1572872 | tf_op jit(solution)/shard_map/ppermute | solution.py:21
  52.0 7.4 %collective-permute-start.9 = (bf16[4,64,1280]{2,1,0:T(8,128)(2,1)}, bf16[4,64,1280]{2,1,0:T(8,128)(2,1)}, u32[]{:S(2)}, u32[]{:S(2)}) collective-permute-start(bf16[4,64,1280]{2,1,0:T(8,128)(2,1)} %all-to-all-done.1.near_ref), channel_id=1, source_target_pairs={{0,1},{1,0},{2,3},{3,2},{4,5},{5,4},{6,7},{7,6},{8,9},{9,8},{10,11... | collective-permute-start | bytes 1966088 | tf_op jit(solution)/shard_map/ppermute | solution.py:21
  52.0 14.0 %collective-permute-start.10 = (bf16[8,64,640]{2,1,0:T(8,128)(2,1)S(1)}, bf16[8,64,640]{2,1,0:T(8,128)(2,1)S(1)}, u32[]{:S(2)}, u32[]{:S(2)}) collective-permute-start(bf16[8,64,640]{2,1,0:T(8,128)(2,1)S(1)} %all-to-all-done.near_ref), channel_id=1, source_target_pairs={{0,1},{1,0},{2,3},{3,2},{4,5},{5,4},{6,7},{7,6},{8,9},{9,8},{10,11... | collective-permute-start | bytes 1966088 | tf_op jit(solution)/shard_map/ppermute | solution.py:21
  59.3 6.7 %collective-permute-start.12 = (bf16[80,1152]{1,0:T(8,128)(2,1)S(1)}, bf16[80,1152]{1,0:T(8,128)(2,1)S(1)}, u32[]{:S(2)}, u32[]{:S(2)}) collective-permute-start(bf16[80,1152]{1,0:T(8,128)(2,1)S(1)} %collective-permute-done.7.refs_5_.refs_13_), channel_id=1, source_target_pairs={{0,16},{16,32},{32,48},{48,64},{64,80},{80,96},{96,112},{112,0},{1... | collective-permute-start | bytes 552968 | tf_op jit(solution)/shard_map/ppermute | solution.py:21
  59.4 15.2 %copy-start.5 = (bf16[256,1024]{1,0:T(8,128)(2,1)S(1)}, bf16[256,1024]{1,0:T(8,128)(2,1)}, u32[]{:S(2)}) copy-start(bf16[256,1024]{1,0:T(8,128)(2,1)} %copy-done.4) | copy-start | bytes 1572868
  70.5 15.4 %collective-permute-start.14 = (bf16[256,1024]{1,0:T(8,128)(2,1)}, bf16[256,1024]{1,0:T(8,128)(2,1)}, u32[]{:S(2)}, u32[]{:S(2)}) collective-permute-start(bf16[256,1024]{1,0:T(8,128)(2,1)} %get-tuple-element.51), channel_id=1, source_target_pairs={{0,8},{4,12},{8,0},{12,4},{1,9},{5,13},{9,1},{13,5},{2,10},{6,14},... | collective-permute-start | bytes 1572872 | tf_op jit(solution)/shard_map/ppermute | solution.py:21
  71.0 19.2 %collective-permute-start.15 = (bf16[256,1024]{1,0:T(8,128)(2,1)}, bf16[256,1024]{1,0:T(8,128)(2,1)}, u32[]{:S(2)}, u32[]{:S(2)}) collective-permute-start(bf16[256,1024]{1,0:T(8,128)(2,1)} %get-tuple-element.52), channel_id=1, source_target_pairs={{0,4},{4,8},{8,12},{12,0},{1,5},{5,9},{9,13},{13,1},{2,6},{6,10},{... | collective-permute-start | bytes 1572872 | tf_op jit(solution)/shard_map/ppermute | solution.py:21
  72.6 17.6 %collective-permute-start.13 = (bf16[256,1024]{1,0:T(8,128)(2,1)}, bf16[256,1024]{1,0:T(8,128)(2,1)}, u32[]{:S(2)}, u32[]{:S(2)}) collective-permute-start(bf16[256,1024]{1,0:T(8,128)(2,1)} %get-tuple-element.49), channel_id=1, source_target_pairs={{0,12},{4,0},{8,4},{12,8},{1,13},{5,1},{9,5},{13,9},{2,14},{6,2},{... | collective-permute-start | bytes 1572872 | tf_op jit(solution)/shard_map/ppermute | solution.py:21
  79.9 34.2 %all-to-all-start.2 = ((bf16[8,80,1024]{2,1,0:T(8,128)(2,1)}), bf16[8,80,1024]{2,1,0:T(8,128)(2,1)}, u32[]{:S(2)}, u32[]{:S(2)}) async-start(bf16[8,80,1024]{2,1,0:T(8,128)(2,1)} %bitcast.14), calls=%async_computation.2 | async-start | bytes 2621440 | tf_op jit(solution)/shard_map/all_to_all | solution.py:379
  92.7 4.5 %collective-permute-start.20 = (bf16[256,128]{1,0:T(8,128)(2,1)}, bf16[256,128]{1,0:T(8,128)(2,1)S(1)}, u32[]{:S(2)}, u32[]{:S(2)}) collective-permute-start(bf16[256,128]{1,0:T(8,128)(2,1)} %get-tuple-element.63.refs_0_), channel_id=1, source_target_pairs={{0,128},{128,0},{1,129},{129,1},{2,130},{130,2},{3,131},{131,3},{4... | collective-permute-start | bytes 196616 | tf_op jit(solution)/shard_map/ppermute | solution.py:21
  92.8 8.5 %collective-permute-start.19 = (bf16[640,128]{1,0:T(8,128)(2,1)S(1)}, bf16[640,128]{1,0:T(8,128)(2,1)S(1)}, u32[]{:S(2)}, u32[]{:S(2)}) collective-permute-start(bf16[640,128]{1,0:T(8,128)(2,1)S(1)} %get-tuple-element.64.refs_0_), channel_id=1, source_target_pairs={{0,12},{4,0},{8,4},{12,8},{1,13},{5,1},{9,5},{13,9},{2,14},{6,2},{... | collective-permute-start | bytes 491528 | tf_op jit(solution)/shard_map/ppermute | solution.py:21
  94.0 7.3 %collective-permute-start.18 = (bf16[640,128]{1,0:T(8,128)(2,1)S(1)}, bf16[640,128]{1,0:T(8,128)(2,1)S(1)}, u32[]{:S(2)}, u32[]{:S(2)}) collective-permute-start(bf16[640,128]{1,0:T(8,128)(2,1)S(1)} %get-tuple-element.64.refs_0_), channel_id=1, source_target_pairs={{0,8},{4,12},{8,0},{12,4},{1,9},{5,13},{9,1},{13,5},{2,10},{6,14},... | collective-permute-start | bytes 491528 | tf_op jit(solution)/shard_map/ppermute | solution.py:21
  96.0 6.6 %collective-permute-start.17 = (bf16[640,128]{1,0:T(8,128)(2,1)S(1)}, bf16[640,128]{1,0:T(8,128)(2,1)S(1)}, u32[]{:S(2)}, u32[]{:S(2)}) collective-permute-start(bf16[640,128]{1,0:T(8,128)(2,1)S(1)} %get-tuple-element.64.refs_0_), channel_id=1, source_target_pairs={{0,4},{4,8},{8,12},{12,0},{1,5},{5,9},{9,13},{13,1},{2,6},{6,10},{... | collective-permute-start | bytes 491528 | tf_op jit(solution)/shard_map/ppermute | solution.py:21
  105.0 4.6 %collective-permute-start.21 = (bf16[2,64,2560]{2,1,0:T(8,128)(2,1)}, bf16[2,64,2560]{2,1,0:T(8,128)(2,1)}, u32[]{:S(2)}, u32[]{:S(2)}) collective-permute-start(bf16[2,64,2560]{2,1,0:T(8,128)(2,1)} %get-tuple-element.68), channel_id=1, source_target_pairs={{0,1},{1,0},{2,3},{3,2},{4,5},{5,4},{6,7},{7,6},{8,9},{9,8},{10,11... | collective-permute-start | bytes 1966088 | tf_op jit(solution)/shard_map/ppermute | solution.py:21
  105.1 12.3 %collective-permute-start.23 = (bf16[8,40,128]{2,1,0:T(8,128)(2,1)}, bf16[8,40,128]{2,1,0:T(8,128)(2,1)S(1)}, u32[]{:S(2)}, u32[]{:S(2)}) collective-permute-start(bf16[8,40,128]{2,1,0:T(8,128)(2,1)} %get-tuple-element.70), channel_id=1, source_target_pairs={{0,4},{4,8},{8,12},{12,0},{1,5},{5,9},{9,13},{13,1},{2,6},{6,10},{... | collective-permute-start | bytes 245768 | tf_op jit(solution)/shard_map/ppermute | solution.py:21
  105.6 11.8 %collective-permute-start.24 = (bf16[8,40,128]{2,1,0:T(8,128)(2,1)}, bf16[8,40,128]{2,1,0:T(8,128)(2,1)}, u32[]{:S(2)}, u32[]{:S(2)}) collective-permute-start(bf16[8,40,128]{2,1,0:T(8,128)(2,1)} %get-tuple-element.71), channel_id=1, source_target_pairs={{0,8},{4,12},{8,0},{12,4},{1,9},{5,13},{9,1},{13,5},{2,10},{6,14},... | collective-permute-start | bytes 245768 | tf_op jit(solution)/shard_map/ppermute | solution.py:21
  107.3 10.1 %collective-permute-start.25 = (bf16[8,40,128]{2,1,0:T(8,128)(2,1)}, bf16[8,40,128]{2,1,0:T(8,128)(2,1)}, u32[]{:S(2)}, u32[]{:S(2)}) collective-permute-start(bf16[8,40,128]{2,1,0:T(8,128)(2,1)} %get-tuple-element.72), channel_id=1, source_target_pairs={{0,12},{4,0},{8,4},{12,8},{1,13},{5,1},{9,5},{13,9},{2,14},{6,2},{... | collective-permute-start | bytes 245768 | tf_op jit(solution)/shard_map/ppermute | solution.py:21
  111.4 17.8 %collective-permute-start.22 = (bf16[64,2560]{1,0:T(8,128)(2,1)}, bf16[64,2560]{1,0:T(8,128)(2,1)}, u32[]{:S(2)}, u32[]{:S(2)}) collective-permute-start(bf16[64,2560]{1,0:T(8,128)(2,1)} %fusion.1), channel_id=1, source_target_pairs={{0,2},{2,0},{1,3},{3,1},{4,6},{6,4},{5,7},{7,5},{8,10},{10,8},{9,1... | collective-permute-start | bytes 983048 | tf_op jit(solution)/shard_map/ppermute | solution.py:21
  115.7 9.2 %collective-permute-start.16 = (bf16[40,1024]{1,0:T(8,128)(2,1)S(1)}, bf16[40,1024]{1,0:T(8,128)(2,1)S(1)}, u32[]{:S(2)}, u32[]{:S(2)}) collective-permute-start(bf16[40,1024]{1,0:T(8,128)(2,1)S(1)} %dynamic-slice_bitcast_fusion), channel_id=1, source_target_pairs={{0,128},{128,0},{1,129},{129,1},{2,130},{130,2},{3,131},{131,3},{4... | collective-permute-start | bytes 245768 | tf_op jit(solution)/shard_map/ppermute | solution.py:21
  119.0 12.9 %all-to-all-start.3 = ((bf16[8,40,128]{2,1,0:T(8,128)(2,1)}), bf16[8,40,128]{2,1,0:T(8,128)(2,1)S(1)}, u32[]{:S(2)}, u32[]{:S(2)}) async-start(bf16[8,40,128]{2,1,0:T(8,128)(2,1)} %add_convert_fusion.1), calls=%async_computation.3 | async-start | bytes 163840 | tf_op jit(solution)/shard_map/all_to_all | solution.py:398
  (12 other events, 65.3 us)
